TPU v7x, 32 devices: a whole 2x2x4 slice. The times are simulated.
32 devices in a mesh: groups: 2 (over x), ctx: 16 (over z, y, core).
Axes of the slice: x: 2, y: 2, z: 4, core: 2. Of those that a mesh axis runs over, the one named last changes fastest.
Arguments:
- rotated_queries: bfloat16 [4096, 2048], P(('groups', 'ctx')), parts along dimension 0, may hold values from -6.5 to 6.5
- key_rows: bfloat16 [4096, 512], P(('groups', 'ctx')), parts along dimension 0, may hold values from -6.5 to 6.5
- value_matrix: bfloat16 [4096, 512], P(('groups', 'ctx')), parts along dimension 0, may hold values from -6 to 6
- doc_lengths: int32 [8], P('groups'), parts along dimension 0, may hold values from 1 to 1024, 2048 in all
Outputs:
- attended: bfloat16 [4096, 2048], P(('groups', 'ctx')), parts along dimension 0
There are 2 independent parts, one for each index of `groups`. A program takes and returns all parts, laid end to end along the dimension named above; each array names one. Nothing has to cross between parts.
Inputs may be any that keep to these rules, and one draw needn't show every extreme that they name: `doc_lengths`: the 4 lengths of one part sum to 2048; the largest is exactly 1024.
All inputs are finite; a program needn't handle non-finite values.
Results may differ from a plain program's by a relative error of at most 0.005.
Values may be sent and summed in bfloat16 or wider, within the bound.
A program may use at most 128 MiB of HBM per device.

v0:
```python
import jax
import jax.numpy as jnp
from jax import lax
from jax.sharding import PartitionSpec as P

QUERY_HEADS = 16
KEY_VALUE_HEADS = 4
HEAD_WIDTH = 128


masked_score = -1e30


def from_behind(shard, axis, by):
    peers = lax.axis_size(axis)
    pairs = [(i, i + by) for i in range(peers) if 0 <= i + by < peers]
    return lax.ppermute(shard, axis, pairs)


def doc_start_of(query_pos, doc_lengths):
    doc_ends = jnp.cumsum(doc_lengths)
    taken_lengths = jnp.where(doc_ends[None, :] <= query_pos[:, None], doc_lengths[None, :], 0)
    return jnp.sum(taken_lengths, axis=1)


def fold_block(state_now, block_slice, key_start, grouped_heads, query_pos, query_start):
    run_max, run_sum, accumulated = state_now
    token_count = block_slice.shape[1]
    local_keys = block_slice[0].reshape(token_count, KEY_VALUE_HEADS, HEAD_WIDTH)
    local_values = block_slice[1].reshape(token_count, KEY_VALUE_HEADS, HEAD_WIDTH)
    scores = jnp.einsum(
        "tkgd,skd->tkgs", grouped_heads, local_keys, preferred_element_type=jnp.float32
    ) * HEAD_WIDTH ** (-0.5)
    key_pos = key_start + jnp.arange(token_count, dtype=jnp.int32)
    allowed = (key_pos[None, :] >= query_start[:, None]) & (key_pos[None, :] <= query_pos[:, None])
    allowed = allowed[:, None, None, :]
    scores = jnp.where(allowed, scores, masked_score)
    new_max = jnp.maximum(run_max, jnp.max(scores, axis=-1))
    weights = jnp.where(allowed, jnp.exp(scores - new_max[..., None]), 0.0)
    factor = jnp.exp(run_max - new_max)
    run_sum = run_sum * factor + jnp.sum(weights, axis=-1)
    accumulated = accumulated * factor[..., None] + jnp.einsum(
        "tkgs,skd->tkgd",
        weights.astype(jnp.bfloat16),
        local_values,
        preferred_element_type=jnp.float32,
    )
    return (new_max, run_sum, accumulated)


def visit_block(state_now, block_slice, key_start, grouped_heads, query_pos, query_start):
    return fold_block(state_now, block_slice, key_start, grouped_heads, query_pos, query_start)


def per_device(rotated_queries, key_rows, value_matrix, doc_lengths):
    count_of_rows = rotated_queries.shape[0]
    span_count = lax.axis_size("ctx") // 2
    device_index = lax.axis_index("ctx")
    query_pos = device_index * count_of_rows + jnp.arange(count_of_rows, dtype=jnp.int32)
    query_start = doc_start_of(query_pos, doc_lengths)
    grouped_heads = rotated_queries.reshape(
        count_of_rows, KEY_VALUE_HEADS, QUERY_HEADS // KEY_VALUE_HEADS, HEAD_WIDTH
    )
    statistic_shape = (count_of_rows, KEY_VALUE_HEADS, QUERY_HEADS // KEY_VALUE_HEADS)
    state_now = (
        jnp.full(statistic_shape, masked_score, jnp.float32),
        jnp.zeros(statistic_shape, jnp.float32),
        jnp.zeros(statistic_shape + (HEAD_WIDTH,), jnp.float32),
    )
    own_block = jnp.stack([key_rows, value_matrix])
    state_now = visit_block(
        state_now, own_block, device_index * count_of_rows, grouped_heads, query_pos, query_start
    )
    stored = own_block[None]
    for level_number in range(16):
        held_count = stored.shape[0]
        send_count = min(held_count, span_count + 1 - held_count)
        if send_count > 0:
            arrived = from_behind(stored[:send_count], "ctx", held_count)

            def arrived_step(offset_number, inner_state, arrived=arrived, held_count=held_count):
                block_slice = lax.dynamic_index_in_dim(arrived, offset_number, 0, keepdims=False)
                key_start = (device_index - held_count - offset_number) * count_of_rows
                return visit_block(
                    inner_state, block_slice, key_start, grouped_heads, query_pos, query_start
                )

            state_now = lax.fori_loop(0, send_count, arrived_step, state_now)
            stored = jnp.concatenate([stored, arrived], axis=0)
    run_max, run_sum, accumulated = state_now
    result = accumulated / run_sum[..., None]
    return result.reshape(count_of_rows, QUERY_HEADS * HEAD_WIDTH).astype(jnp.bfloat16)


def solution(mesh):
    in_specs = (
        P(("groups", "ctx"), None),
        P(("groups", "ctx"), None),
        P(("groups", "ctx"), None),
        P("groups"),
    )
    out_specs = P(("groups", "ctx"), None)
    return jax.shard_map(
        per_device, mesh=mesh, in_specs=in_specs, out_specs=out_specs, check_vma=False
    )
```

profile of v0, /device:TPU:16, one launch (start us, length us, event | category | flops | bytes accessed | tf_op | source)
XLA Modules:
  0.0 72.0 jit_solution(6056513626259436427)
XLA Ops:
  0.0 1.1 %copy.46 = bf16[128,512]{0,1:T(8,128)(2,1)S(1)} copy(bf16[128,512]{1,0:T(8,128)(2,1)} %param.9) | data formatting | bytes 262144 | tf_op args[1]
  1.1 0.0 copy-start.2
  1.1 0.1 copy.47
  1.2 0.0 copy-start.1
  1.3 2.1 %collective-permute-start = (bf16[1,2,128,512]{2,3,1,0:T(8,128)(2,1)S(1)}, bf16[1,2,128,512]{2,3,1,0:T(8,128)(2,1)S(1)}, u32[]{:S(2)}, u32[]{:S(2)}) collective-permute-start(bf16[1,2,128,512]{2,3,1,0:T(8,128)(2,1)S(1)} %maximum_bitcast_fusion), channel_id=1, source_target_pairs={{0,1},{1,2},{2,3},{3,4},{4,5},{5,6},{6,7},{7,8},{8,9},{9,10},{10,1... | collective-permute-start | bytes 786440 | tf_op jit(solution)/shard_map/ppermute | solution.py:17
  3.3 1.3 %collective-permute-start.3 = (bf16[1,2,128,512]{2,3,1,0:T(8,128)(2,1)S(1)}, bf16[1,2,128,512]{2,3,1,0:T(8,128)(2,1)S(1)}, u32[]{:S(2)}, u32[]{:S(2)}) collective-permute-start(bf16[1,2,128,512]{2,3,1,0:T(8,128)(2,1)S(1)} %maximum_bitcast_fusion), channel_id=1, source_target_pairs={{0,8},{1,9},{2,10},{3,11},{4,12},{5,13},{6,14},{7,15},{16,24},{17,... | collective-permute-start | bytes 786440 | tf_op jit(solution)/shard_map/ppermute | solution.py:17
  4.7 0.0 copy-start.8
  4.7 0.6 copy-done.8
  5.4 0.2 reduce-window.8
  5.6 0.3 copy.43
  5.8 0.3 copy.55
  6.2 0.1 select_reduce_fusion
  6.2 0.7 compare_and_fusion.2
  6.9 0.3 fusion.63
  7.3 2.7 %collective-permute-done = bf16[1,2,128,512]{2,3,1,0:T(8,128)(2,1)S(1)} collective-permute-done((bf16[1,2,128,512]{2,3,1,0:T(8,128)(2,1)S(1)}, bf16[1,2,128,512]{2,3,1,0:T(8,128)(2,1)S(1)}, u32[]{:S(2)}, u32[]{:S(2)}) %collective-permute-start) | collective-permute-done | bytes 262176 | tf_op jit(solution)/shard_map/ppermute | solution.py:17
  10.0 0.8 %pad_maximum_fusion.1 = bf16[2,2,128,512]{2,3,1,0:T(8,128)(2,1)} fusion(bf16[1,2,128,512]{2,3,1,0:T(8,128)(2,1)S(1)} %collective-permute-done, bf16[1,2,128,512]{2,3,1,0:T(8,128)(2,1)S(1)} %maximum_bitcast_fusion), kind=kLoop, calls=%fused_computation.66 | loop fusion | flops 262144 | bytes 1048576 | tf_op jit(solution)/shard_map/concatenate | solution.py:89
  10.8 2.5 %collective-permute-start.1 = (bf16[2,2,128,512]{2,3,1,0:T(8,128)(2,1)}, bf16[2,2,128,512]{2,3,1,0:T(8,128)(2,1)S(1)}, u32[]{:S(2)}, u32[]{:S(2)}) collective-permute-start(bf16[2,2,128,512]{2,3,1,0:T(8,128)(2,1)} %pad_maximum_fusion.1), channel_id=1, source_target_pairs={{0,2},{1,3},{2,4},{3,5},{4,6},{5,7},{6,8},{7,9},{8,10},{9,11},{10,... | collective-permute-start | bytes 1572872 | tf_op jit(solution)/shard_map/ppermute | solution.py:17
  13.4 0.4 fusion.64
  13.8 0.4 fusion.34
  14.2 0.8 %fusion.28 = f32[128,4,4,128]{3,0,2,1:T(8,128)S(1)} fusion(f32[128,4,4,128]{0,3,2,1:T(8,128)S(1)} %get-tuple-element.655, f32[128,4,4]{0,2,1:T(4,128)S(1)} %get-tuple-element.631, f32[128,4,4]{0,2,1:T(4,128)S(1)} %get-tuple-element.648, f32[128,4,4]{0,2,1:T(4,128)S(1)} %get-tuple-element.650, pred[128,128]{0,1:T(8,128)(4,1)S(1)} %get-tuple-element.652, ...), kind=kOutput, calls=%fused_computation.48 | convolution fusion | flops 68419584 | bytes 2269184 | tf_op jit(solution)/shard_map/tkgs,skd->tkgd/dot_general | solution.py:42
  15.1 1.4 %fusion.26 = f32[128,4,4,128]{3,0,2,1:T(8,128)} fusion(f32[128,4,4,128]{3,0,2,1:T(8,128)S(1)} %fusion.28, bf16[128,4,128,1]{0,2,3,1:T(8,128)(2,1)S(1)} %bitcast.195, f32[128,4,4,128]{0,3,2,1:T(8,128)S(1)} %get-tuple-element.657, f32[128,4,4]{0,2,1:T(4,128)S(1)} %get-tuple-element.815, pred[128,128]{0,1:T(8,128)(4,1)S(1)} %get-tuple-element.653), kind=kOutput, calls=%fused_computation.45 | convolution fusion | flops 68157440 | bytes 3301376 | tf_op jit(solution)/shard_map/while/body/eval_jaxpr/tkgs,skd->tkgd/dot_general | solution.py:42
  16.4 1.6 %copy.54 = f32[128,4,4,128]{0,3,2,1:T(8,128)S(1)} copy(f32[128,4,4,128]{3,0,2,1:T(8,128)} %fusion.26) | data formatting | bytes 2097152
  18.0 0.0 collective-permute-done.3
  18.0 0.7 fusion.61
  18.7 0.0 copy-done.4
  18.7 1.4 %fusion.65 = (f32[128,4,4]{0,2,1:T(4,128)S(1)}, f32[128,4,4,128]{0,3,2,1:T(8,128)}) fusion(bf16[128,4,128,1]{0,2,3,1:T(8,128)(2,1)S(1)} %bitcast.199, bf16[128,4,4,128]{0,3,2,1:T(8,128)(2,1)S(1)} %bitcast.174, pred[128,128]{0,1:T(8,128)(4,1)S(1)} %copy-done.4), kind=kOutput, calls=%fused_computation.102 | convolution fusion | flops 67893248 | bytes 1728512 | tf_op jit(solution)/shard_map/while/body/eval_jaxpr/tkgd,skd->tkgs/dot_general | solution.py:31
  20.1 12.4 %collective-permute-done.1 = bf16[2,2,128,512]{2,3,1,0:T(8,128)(2,1)S(1)} collective-permute-done((bf16[2,2,128,512]{2,3,1,0:T(8,128)(2,1)}, bf16[2,2,128,512]{2,3,1,0:T(8,128)(2,1)S(1)}, u32[]{:S(2)}, u32[]{:S(2)}) %collective-permute-start.1) | collective-permute-done | bytes 524320 | tf_op jit(solution)/shard_map/ppermute | solution.py:17
  32.5 1.1 %pad_maximum_fusion = bf16[4,2,128,512]{2,3,1,0:T(8,128)(2,1)} fusion(bf16[2,2,128,512]{2,3,1,0:T(8,128)(2,1)S(1)} %collective-permute-done.1, bf16[1,2,128,512]{2,3,1,0:T(8,128)(2,1)S(1)} %collective-permute-done, bf16[1,2,128,512]{2,3,1,0:T(8,128)(2,1)S(1)} %maximum_bitcast_fusion), kind=kLoop, calls=%fused_computation.55 | loop fusion | flops 1048576 | bytes 2097152 | tf_op jit(solution)/shard_map/concatenate | solution.py:89
  33.6 2.5 %collective-permute-start.2 = (bf16[4,2,128,512]{2,3,1,0:T(8,128)(2,1)}, bf16[4,2,128,512]{2,3,1,0:T(8,128)(2,1)}, u32[]{:S(2)}, u32[]{:S(2)}) collective-permute-start(bf16[4,2,128,512]{2,3,1,0:T(8,128)(2,1)} %pad_maximum_fusion), channel_id=1, source_target_pairs={{0,4},{1,5},{2,6},{3,7},{4,8},{5,9},{6,10},{7,11},{8,12},{9,13},{1... | collective-permute-start | bytes 3145736 | tf_op jit(solution)/shard_map/ppermute | solution.py:17
  36.1 2.8 %while.26 = (s32[]{:T(128)}, f32[128,4,4]{0,2,1:T(4,128)S(1)}, f32[128,4,4]{0,2,1:T(4,128)S(1)}, f32[128,4,4,128]{0,3,2,1:T(8,128)S(1)}, s32[]{:T(128)}, /*index...) while((s32[]{:T(128)}, f32[128,4,4]{0,2,1:T(4,128)S(1)}, ...), condition=%wide.region_9.10_spmd.clone, body=%wide.region_6.9_spmd.clone.sunk | while | flops 137154816 | bytes 6752945 | solution.py:88
  36.2 0.1 compare_and_fusion.7
  36.3 0.4 fusion.97
  36.7 0.2 fusion.98
  36.9 0.6 fusion.99
  37.6 0.1 compare_and_fusion.7
  37.7 0.4 fusion.97
  38.1 0.2 fusion.98
  38.3 0.6 fusion.99
  38.9 21.3 %collective-permute-done.2 = bf16[4,2,128,512]{2,3,1,0:T(8,128)(2,1)} collective-permute-done((bf16[4,2,128,512]{2,3,1,0:T(8,128)(2,1)}, bf16[4,2,128,512]{2,3,1,0:T(8,128)(2,1)}, u32[]{:S(2)}, u32[]{:S(2)}) %collective-permute-start.2) | collective-permute-done | bytes 1048608 | tf_op jit(solution)/shard_map/ppermute | solution.py:17
  60.3 9.5 %while.27 = (s32[]{:T(128)}, f32[128,4,4]{0,2,1:T(4,128)S(1)}, f32[128,4,4]{0,2,1:T(4,128)S(1)}, f32[128,4,4,128]{0,3,2,1:T(8,128)S(1)}, s32[]{:T(128)}, /*index...) while((s32[]{:T(128)}, f32[128,4,4]{0,2,1:T(4,128)S(1)}, ...), condition=%wide.region_13.14_spmd.clone, body=%wide.region_10.13_spmd.clone.sunk | while | flops 137154816 | bytes 6752945 | solution.py:88
  60.3 0.1 compare_and_fusion.8
  60.4 1.1 %constant_dynamic-slice_fusion.7 = (bf16[1,1,128,512]{2,3,1,0:T(8,128)(2,1)S(1)}, bf16[1,1,128,512]{2,3,1,0:T(8,128)(2,1)S(1)}) fusion(bf16[4,2,128,512]{2,3,1,0:T(8,128)(2,1)} %get-tuple-element.885, s32[]{:T(128)} %get-tuple-element.866, s32[]{:T(128)S(6)} %add.300), kind=kLoop, calls=%fused_computation.37.clone.1 | loop fusion | bytes 524296 | tf_op jit(solution)/shard_map/while/body/eval_jaxpr/slice | solution.py:30
  61.4 0.4 fusion.104
  61.8 0.2 fusion.105
  62.1 0.6 fusion.106
  62.7 0.1 compare_and_fusion.8
  62.8 1.0 %constant_dynamic-slice_fusion.7 = (bf16[1,1,128,512]{2,3,1,0:T(8,128)(2,1)S(1)}, bf16[1,1,128,512]{2,3,1,0:T(8,128)(2,1)S(1)}) fusion(bf16[4,2,128,512]{2,3,1,0:T(8,128)(2,1)} %get-tuple-element.885, s32[]{:T(128)} %get-tuple-element.866, s32[]{:T(128)S(6)} %add.300), kind=kLoop, calls=%fused_computation.37.clone.1 | loop fusion | bytes 524296 | tf_op jit(solution)/shard_map/while/body/eval_jaxpr/slice | solution.py:30
  63.8 0.4 fusion.104
  64.2 0.2 fusion.105
  64.4 0.6 fusion.106
  65.1 0.1 compare_and_fusion.8
  65.2 1.0 %constant_dynamic-slice_fusion.7 = (bf16[1,1,128,512]{2,3,1,0:T(8,128)(2,1)S(1)}, bf16[1,1,128,512]{2,3,1,0:T(8,128)(2,1)S(1)}) fusion(bf16[4,2,128,512]{2,3,1,0:T(8,128)(2,1)} %get-tuple-element.885, s32[]{:T(128)} %get-tuple-element.866, s32[]{:T(128)S(6)} %add.300), kind=kLoop, calls=%fused_computation.37.clone.1 | loop fusion | bytes 524296 | tf_op jit(solution)/shard_map/while/body/eval_jaxpr/slice | solution.py:30
  66.2 0.4 fusion.104
  66.6 0.2 fusion.105
  66.8 0.6 fusion.106
  67.4 0.1 compare_and_fusion.8
  67.5 1.0 %constant_dynamic-slice_fusion.7 = (bf16[1,1,128,512]{2,3,1,0:T(8,128)(2,1)S(1)}, bf16[1,1,128,512]{2,3,1,0:T(8,128)(2,1)S(1)}) fusion(bf16[4,2,128,512]{2,3,1,0:T(8,128)(2,1)} %get-tuple-element.885, s32[]{:T(128)} %get-tuple-element.866, s32[]{:T(128)S(6)} %add.300), kind=kLoop, calls=%fused_computation.37.clone.1 | loop fusion | bytes 524296 | tf_op jit(solution)/shard_map/while/body/eval_jaxpr/slice | solution.py:30
  68.5 0.4 fusion.104
  68.9 0.2 fusion.105
  69.1 0.6 fusion.106
  69.8 0.2 fusion.37
  70.0 0.7 copy-done.5
  70.7 0.3 divide_convert_fusion
  71.0 1.0 %copy.60 = bf16[128,2048]{1,0:T(8,128)(2,1)} copy(bf16[128,2048]{0,1:T(8,128)(2,1)S(1)} %bitcast.194) | data formatting | bytes 1048576 | tf_op jit(solution)/shard_map/convert_element_type | solution.py:92
  (49 shorter events, 0.4 us)
Async XLA Ops:
  0.0 1.1 %copy-start.3 = (bf16[128,512]{1,0:T(8,128)(2,1)S(1)}, bf16[128,512]{1,0:T(8,128)(2,1)}, u32[]{:S(2)}) copy-start(bf16[128,512]{1,0:T(8,128)(2,1)} %param.10) | copy-start | bytes 393220
  1.1 3.5 %copy-start.2 = (bf16[128,512]{1,0:T(8,128)(2,1)S(1)}, bf16[128,512]{1,0:T(8,128)(2,1)}, u32[]{:S(2)}) copy-start(bf16[128,512]{1,0:T(8,128)(2,1)} %param.9) | copy-start | bytes 393220
  1.2 4.4 %copy-start.1 = (bf16[128,2048]{1,0:T(8,128)(2,1)S(1)}, bf16[128,2048]{1,0:T(8,128)(2,1)}, u32[]{:S(2)}) copy-start(bf16[128,2048]{1,0:T(8,128)(2,1)} %param.8) | copy-start | bytes 1572868
  1.3 8.7 %collective-permute-start = (bf16[1,2,128,512]{2,3,1,0:T(8,128)(2,1)S(1)}, bf16[1,2,128,512]{2,3,1,0:T(8,128)(2,1)S(1)}, u32[]{:S(2)}, u32[]{:S(2)}) collective-permute-start(bf16[1,2,128,512]{2,3,1,0:T(8,128)(2,1)S(1)} %maximum_bitcast_fusion), channel_id=1, source_target_pairs={{0,1},{1,2},{2,3},{3,4},{4,5},{5,6},{6,7},{7,8},{8,9},{9,10},{10,1... | collective-permute-start | bytes 786440 | tf_op jit(solution)/shard_map/ppermute | solution.py:17
  3.3 14.7 %collective-permute-start.3 = (bf16[1,2,128,512]{2,3,1,0:T(8,128)(2,1)S(1)}, bf16[1,2,128,512]{2,3,1,0:T(8,128)(2,1)S(1)}, u32[]{:S(2)}, u32[]{:S(2)}) collective-permute-start(bf16[1,2,128,512]{2,3,1,0:T(8,128)(2,1)S(1)} %maximum_bitcast_fusion), channel_id=1, source_target_pairs={{0,8},{1,9},{2,10},{3,11},{4,12},{5,13},{6,14},{7,15},{16,24},{17,... | collective-permute-start | bytes 786440 | tf_op jit(solution)/shard_map/ppermute | solution.py:17
  4.7 0.7 copy-start.8
  6.2 0.7 copy-start.6
  10.8 21.7 %collective-permute-start.1 = (bf16[2,2,128,512]{2,3,1,0:T(8,128)(2,1)}, bf16[2,2,128,512]{2,3,1,0:T(8,128)(2,1)S(1)}, u32[]{:S(2)}, u32[]{:S(2)}) collective-permute-start(bf16[2,2,128,512]{2,3,1,0:T(8,128)(2,1)} %pad_maximum_fusion.1), channel_id=1, source_target_pairs={{0,2},{1,3},{2,4},{3,5},{4,6},{5,7},{6,8},{7,9},{8,10},{9,11},{10,... | collective-permute-start | bytes 1572872 | tf_op jit(solution)/shard_map/ppermute | solution.py:17
  18.0 0.7 copy-start.4
  33.6 2.5 %copy-start.7 = (s32[128]{0:T(128)S(1)}, s32[128]{0:T(128)}, u32[]{:S(2)}) copy-start(s32[128]{0:T(128)} %copy-done.6) | copy-start | bytes 1540
  33.6 26.7 %collective-permute-start.2 = (bf16[4,2,128,512]{2,3,1,0:T(8,128)(2,1)}, bf16[4,2,128,512]{2,3,1,0:T(8,128)(2,1)}, u32[]{:S(2)}, u32[]{:S(2)}) collective-permute-start(bf16[4,2,128,512]{2,3,1,0:T(8,128)(2,1)} %pad_maximum_fusion), channel_id=1, source_target_pairs={{0,4},{1,5},{2,6},{3,7},{4,8},{5,9},{6,10},{7,11},{8,12},{9,13},{1... | collective-permute-start | bytes 3145736 | tf_op jit(solution)/shard_map/ppermute | solution.py:17
  60.3 9.5 %copy-start = (f32[128,4,4,128]{0,3,2,1:T(8,128)S(1)}, f32[128,4,4,128]{0,3,2,1:T(8,128)}, u32[]{:S(2)}) copy-start(f32[128,4,4,128]{0,3,2,1:T(8,128)} %get-tuple-element.659) | copy-start | bytes 3145732
  69.8 0.9 %copy-start.5 = (bf16[1,1,128,512]{2,3,1,0:T(8,128)(2,1)S(1)}, bf16[1,1,128,512]{2,3,1,0:T(8,128)(2,1)}, u32[]{:S(2)}) copy-start(bf16[1,1,128,512]{2,3,1,0:T(8,128)(2,1)} %get-tuple-element.645) | copy-start | bytes 393220
where the time goes:
time: 72.4 us; the launch traced here: 72 us
  waiting for transfers between devices  36.5 us (50%)
  local copies, waits for them, and re-layouts  10.6 us (15%)
  matrix products  10.4 us (14%)
  starting transfers between devices  8.39 us (12%)
  other arithmetic  5.49 us (8%)
    ppermute x4, waiting for transfers between devices, from_behind(): return lax.ppermute(shard, axis, pairs)  36.5 us
    ppermute x4, starting transfers between devices, from_behind(): return lax.ppermute(shard, axis, pairs)  8.39 us
    dot_general x9, matrix products, fold_block(): jnp.einsum('tkgs,skd->tkgd', weights.astype(jnp.bfloat16), local_values,...  6.11 us
    unnamed x23, local copies, waits for them, and re-layouts  4.69 us
    dot_general x9, matrix products, fold_block(): jnp.einsum('tkgd,skd->tkgs', grouped_heads, local_keys, preferred_element...  4.32 us
    slice x7, local copies, waits for them, and re-layouts, fold_block(): block_slice[1].reshape(token_count, KEY_VALUE_HEADS, HEAD_WIDTH)  4.12 us
    concatenate x2, other arithmetic, per_device(): stored = jnp.concatenate([stored, arrived], axis=0)  1.93 us
    reduce_sum x8, other arithmetic, fold_block(): run_sum = run_sum * factor + jnp.sum(weights, axis=-1)  1.88 us
  transfers between devices with their start and end apart: 4, of which 3 were waited for; matrix products, arithmetic and copies ran while one was open for 17% of the time, Pallas kernels for 0%

commit v1 on v0

--- a/solution.py
+++ b/solution.py
@@ -1,6 +1,10 @@
+import math
+
 import jax
 import jax.numpy as jnp
 from jax import lax
+from jax.experimental import pallas as pl
+from jax.experimental.pallas import tpu as pltpu
 from jax.sharding import PartitionSpec as P
 
 QUERY_HEADS = 16
@@ -92,6 +96,345 @@
     return result.reshape(count_of_rows, QUERY_HEADS * HEAD_WIDTH).astype(jnp.bfloat16)
 
 
+MESH = pl.DeviceIdType.MESH
+GROUP_HEADS = QUERY_HEADS // KEY_VALUE_HEADS
+EXP2_SCALE = math.log2(math.e) / math.sqrt(HEAD_WIDTH)
+
+(Z1, Z2, C0, Y0, C0Y, C1, Y1, C1Y, C2, Y2, C2Y) = range(11)
+HOPS = 11
+
+
+def relay_kernel(
+    lengths, q_hbm, k_hbm, v_hbm, o_hbm,
+    held, q_rows, q_cols, row_max, row_sum, total, o_rows,
+    own_sem, q_sem, o_sem, send_sem, recv_sem,
+):
+    tokens = q_hbm.shape[0]
+    lanes = GROUP_HEADS * tokens
+    group = lax.axis_index("groups")
+    me = lax.axis_index("ctx")
+    z, y, c = me // 4, (me // 2) % 2, me % 2
+    up, down = me + 4, me - 4
+    across = me + 2 - 4 * y
+    twin = me + 1 - 2 * c
+
+    def place(device):
+        return (group, device)
+
+    def slot(behind, head, from_y, from_c):
+        return held.at[behind, head, from_y, :, from_c]
+
+    def own_copies(head):
+        columns = pl.ds(head * HEAD_WIDTH, HEAD_WIDTH)
+        return [
+            pltpu.make_async_copy(source.at[:, columns], held.at[0, head, y, which, c], own_sem.at[which, head])
+            for which, source in enumerate((k_hbm, v_hbm))
+        ]
+
+    def hop(kind, head, source, target, device):
+        return pltpu.make_async_remote_copy(
+            src_ref=source, dst_ref=target, send_sem=send_sem.at[kind, head],
+            recv_sem=recv_sem.at[kind, head], device_id=place(device), device_id_type=MESH,
+        )
+
+    def send(kind, head, behind, from_y, from_c, device, landing=None):
+        landing = behind if landing is None else landing
+        hop(kind, head, slot(behind, head, from_y, from_c), slot(landing, head, from_y, from_c), device).start()
+
+    def arrived(kind, head, behind, from_y, from_c):
+        here = slot(behind, head, from_y, from_c)
+        hop(kind, head, here, here, twin).wait_recv()
+
+    q_copy = pltpu.make_async_copy(q_hbm, q_rows, q_sem)
+    for head in range(KEY_VALUE_HEADS):
+        for copy in own_copies(head):
+            copy.start()
+    q_copy.start()
+
+    barrier = pltpu.get_barrier_semaphore()
+
+    def greet(device):
+        pl.semaphore_signal(barrier, inc=1, device_id=place(device), device_id_type=MESH)
+
+    greet(twin)
+    greet(across)
+
+    @pl.when(z < 3)
+    def _():
+        greet(up)
+
+    @pl.when(z > 0)
+    def _():
+        greet(down)
+
+    inner = (z > 0) & (z < 3)
+
+    @pl.when(inner)
+    def _():
+        pl.semaphore_wait(barrier, 4)
+
+    @pl.when(jnp.logical_not(inner))
+    def _():
+        pl.semaphore_wait(barrier, 3)
+
+    for head in range(KEY_VALUE_HEADS):
+        for copy in own_copies(head):
+            copy.wait()
+
+        @pl.when(z < 3)
+        def _():
+            send(Z1, head, 0, y, c, up, landing=1)
+
+        @pl.when(y == 0)
+        def _():
+            send(Y0, head, 0, y, c, across)
+
+        @pl.when(c == 0)
+        def _():
+            send(C0, head, 0, y, c, twin)
+
+    q_copy.wait()
+    for head in range(QUERY_HEADS):
+        rows = q_rows[:, head * HEAD_WIDTH:(head + 1) * HEAD_WIDTH].astype(jnp.float32)
+        at = head % GROUP_HEADS
+        q_cols[head // GROUP_HEADS, :, at * tokens:(at + 1) * tokens] = rows.T.astype(jnp.bfloat16)
+
+    query_pos = me * tokens + lax.broadcasted_iota(jnp.int32, (1, lanes), 1) % tokens
+    doc_end = jnp.int32(0)
+    query_start = jnp.zeros((1, lanes), jnp.int32)
+    for doc in range(lengths.shape[0]):
+        doc_end = doc_end + lengths[doc]
+        query_start = query_start + jnp.where(doc_end <= query_pos, lengths[doc], 0)
+
+    half = lanes // 2
+
+    def attend(head, behind, from_y, from_c, pair, own=False):
+        if pair:
+            keys = held[behind, head, from_y, 0].reshape(2 * tokens, HEAD_WIDTH)
+            values = held[behind, head, from_y, 1].reshape(2 * tokens, HEAD_WIDTH)
+        else:
+            keys = held[behind, head, from_y, 0, from_c]
+            values = held[behind, head, from_y, 1, from_c]
+        count = keys.shape[0]
+        key_start = ((z - behind) * 4 + from_y * 2 + (0 if pair else from_c)) * tokens
+        key_pos = key_start + lax.broadcasted_iota(jnp.int32, (count, half), 0)
+        for part in range(2):
+            cols = slice(part * half, (part + 1) * half)
+            scores = jnp.dot(keys, q_cols[head, :, cols], preferred_element_type=jnp.float32)
+            allowed = key_pos >= query_start[:, cols]
+            if own:
+                allowed = allowed & (key_pos <= query_pos[:, cols])
+            scores = jnp.where(allowed, scores, masked_score)
+            new_max = jnp.max(scores, axis=0, keepdims=True)
+            if not own:
+                old_max = row_max[head, :, cols]
+                new_max = jnp.maximum(old_max, new_max)
+            weights = jnp.exp2((scores - new_max) * EXP2_SCALE)
+            weight_sum = jnp.sum(weights, axis=0, keepdims=True)
+            mixed = lax.dot_general(
+                values, weights.astype(jnp.bfloat16), (((0,), (0,)), ((), ())),
+                preferred_element_type=jnp.float32,
+            )
+            if own:
+                row_sum[head, :, cols] = weight_sum
+                total[head, :, cols] = mixed
+            else:
+                factor = jnp.exp2((old_max - new_max) * EXP2_SCALE)
+                row_sum[head, :, cols] = row_sum[head, :, cols] * factor + weight_sum
+                total[head, :, cols] = total[head, :, cols] * factor + mixed
+            row_max[head, :, cols] = new_max
+
+    @pl.loop(0, KEY_VALUE_HEADS)
+    def _(head):
+        attend(head, 0, y, c, False, own=True)
+
+    @pl.loop(0, KEY_VALUE_HEADS + 1)
+    def _(step):
+        @pl.when(step < KEY_VALUE_HEADS)
+        def _():
+            @pl.when(z >= 1)
+            def _():
+                arrived(Z1, step, 1, y, c)
+
+                @pl.when(z < 3)
+                def _():
+                    send(Z2, step, 1, y, c, up, landing=2)
+
+                send(Y1, step, 1, y, c, across)
+                send(C1, step, 1, y, c, twin)
+
+            @pl.when(y == 1)
+            def _():
+                arrived(Y0, step, 0, 0, c)
+                send(C0Y, step, 0, 0, c, twin)
+
+        @pl.when(step >= 1)
+        def _():
+            head = step - 1
+
+            @pl.when(c == 1)
+            def _():
+                arrived(C0, head, 0, y, 0)
+                attend(head, 0, y, 0, False)
+
+            @pl.when(y == 1)
+            def _():
+                arrived(C0Y, head, 0, 0, 1 - c)
+                attend(head, 0, 0, 0, True)
+
+            @pl.when(z >= 1)
+            def _():
+                arrived(C1, head, 1, y, 1 - c)
+                attend(head, 1, y, 0, True)
+
+    @pl.loop(0, KEY_VALUE_HEADS + 1)
+    def _(step):
+        @pl.when(step < KEY_VALUE_HEADS)
+        def _():
+            @pl.when(z >= 1)
+            def _():
+                arrived(Y1, step, 1, 1 - y, c)
+                send(C1Y, step, 1, 1 - y, c, twin)
+
+            @pl.when(z >= 2)
+            def _():
+                arrived(Z2, step, 2, y, c)
+
+                @pl.when(y == 1)
+                def _():
+                    send(Y2, step, 2, y, c, across)
+
+                @pl.when(c == 1)
+                def _():
+                    send(C2, step, 2, y, c, twin)
+
+        @pl.when(step >= 1)
+        def _():
+            head = step - 1
+
+            @pl.when(z >= 1)
+            def _():
+                arrived(C1Y, head, 1, 1 - y, 1 - c)
+                attend(head, 1, 1 - y, 0, True)
+
+            @pl.when(z >= 2)
+            def _():
+                attend(head, 2, y, c, False)
+
+                @pl.when(c == 0)
+                def _():
+                    arrived(C2, head, 2, y, 1)
+                    attend(head, 2, y, 1, False)
+
+    def o_copy(head):
+        columns = pl.ds(pl.multiple_of(head * lanes, lanes), lanes)
+        return pltpu.make_async_copy(o_rows.at[head], o_hbm.at[:, columns], o_sem.at[head])
+
+    from_across = (z >= 2) & (y == 0)
+
+    @pl.loop(0, KEY_VALUE_HEADS + 1)
+    def _(step):
+        @pl.when((step < KEY_VALUE_HEADS) & from_across)
+        def _():
+            arrived(Y2, step, 2, 1, c)
+            send(C2Y, step, 2, 1, c, twin)
+
+        @pl.when(step >= 1)
+        def _():
+            head = step - 1
+
+            @pl.when(from_across)
+            def _():
+                arrived(C2Y, head, 2, 1, 1 - c)
+                attend(head, 2, 1, 0, True)
+
+            result = total[head] / row_sum[head]
+            for at in range(GROUP_HEADS):
+                own_cols = slice(at * tokens, (at + 1) * tokens)
+                o_rows[head, :, at * HEAD_WIDTH:(at + 1) * HEAD_WIDTH] = result[:, own_cols].T.astype(jnp.bfloat16)
+            o_copy(head).start()
+
+    @pl.loop(0, KEY_VALUE_HEADS)
+    def _(head):
+        o_copy(head).wait()
+
+        def sent(kind, behind, from_y, from_c):
+            here = slot(behind, head, from_y, from_c)
+            hop(kind, head, here, here, twin).wait_send()
+
+        @pl.when(z < 3)
+        def _():
+            sent(Z1, 0, y, c)
+
+        @pl.when(y == 0)
+        def _():
+            sent(Y0, 0, y, c)
+
+        @pl.when(c == 0)
+        def _():
+            sent(C0, 0, y, c)
+
+        @pl.when(y == 1)
+        def _():
+            sent(C0Y, 0, 0, c)
+
+        @pl.when(z >= 1)
+        def _():
+            @pl.when(z < 3)
+            def _():
+                sent(Z2, 1, y, c)
+
+            sent(Y1, 1, y, c)
+            sent(C1, 1, y, c)
+            sent(C1Y, 1, 1 - y, c)
+
+        @pl.when((z >= 2) & (y == 1))
+        def _():
+            sent(Y2, 2, y, c)
+
+        @pl.when((z >= 2) & (c == 1))
+        def _():
+            sent(C2, 2, y, c)
+
+        @pl.when(from_across)
+        def _():
+            sent(C2Y, 2, 1, c)
+
+
+def relay_attention(rotated_queries, key_rows, value_matrix, doc_lengths):
+    tokens = rotated_queries.shape[0]
+    lanes = GROUP_HEADS * tokens
+    anywhere = pl.BlockSpec(memory_space=pl.ANY)
+    pairs = 9 * tokens * tokens * QUERY_HEADS
+    return pl.pallas_call(
+        relay_kernel,
+        out_shape=jax.ShapeDtypeStruct(rotated_queries.shape, jnp.bfloat16),
+        in_specs=[pl.BlockSpec(memory_space=pltpu.SMEM), anywhere, anywhere, anywhere],
+        out_specs=anywhere,
+        scratch_shapes=[
+            pltpu.VMEM((3, KEY_VALUE_HEADS, 2, 2, 2, tokens, HEAD_WIDTH), jnp.bfloat16),
+            pltpu.VMEM(rotated_queries.shape, jnp.bfloat16),
+            pltpu.VMEM((KEY_VALUE_HEADS, HEAD_WIDTH, lanes), jnp.bfloat16),
+            pltpu.VMEM((KEY_VALUE_HEADS, 1, lanes), jnp.float32),
+            pltpu.VMEM((KEY_VALUE_HEADS, 1, lanes), jnp.float32),
+            pltpu.VMEM((KEY_VALUE_HEADS, HEAD_WIDTH, lanes), jnp.float32),
+            pltpu.VMEM((KEY_VALUE_HEADS, tokens, GROUP_HEADS * HEAD_WIDTH), jnp.bfloat16),
+            pltpu.SemaphoreType.DMA((2, KEY_VALUE_HEADS)),
+            pltpu.SemaphoreType.DMA,
+            pltpu.SemaphoreType.DMA((KEY_VALUE_HEADS,)),
+            pltpu.SemaphoreType.DMA((HOPS, KEY_VALUE_HEADS)),
+            pltpu.SemaphoreType.DMA((HOPS, KEY_VALUE_HEADS)),
+        ],
+        compiler_params=pltpu.CompilerParams(
+            collective_id=0, has_side_effects=True, vmem_limit_bytes=32 * 1024 * 1024
+        ),
+        cost_estimate=pl.CostEstimate(
+            flops=4 * pairs * HEAD_WIDTH, bytes_accessed=4 * 1024 * 1024, transcendentals=pairs
+        ),
+        name="relay_attention",
+    )(doc_lengths, rotated_queries, key_rows, value_matrix)
+
+
 def solution(mesh):
     in_specs = (
         P(("groups", "ctx"), None),
@@ -100,6 +443,7 @@
         P("groups"),
     )
     out_specs = P(("groups", "ctx"), None)
+    body = relay_attention if mesh.shape["ctx"] == 16 else per_device
     return jax.shard_map(
-        per_device, mesh=mesh, in_specs=in_specs, out_specs=out_specs, check_vma=False
-    )
+        body, mesh=mesh, in_specs=in_specs, out_specs=out_specs, check_vma=False
+    )

time: 72.4 us -> 29.2 us (0.40)
  the two profiles are of different devices: /device:TPU:16 before, /device:TPU:17 now
where the time goes in v1:
time: 29.2 us; the launch traced here: 29 us
  Pallas kernels  24.7 us (85%)
  local copies, waits for them, and re-layouts  4.3 us (15%)
    pallas_call x1, Pallas kernels, relay_attention(): pl.pallas_call(relay_kernel, out_shape=jax.ShapeDtypeStruct(rotated_queri...  24.7 us
    unnamed x9, local copies, waits for them, and re-layouts  4.3 us

profile of v1, /device:TPU:17, one launch (start us, length us, event | category | flops | bytes accessed | tf_op | source)
XLA Modules:
  0.0 29.0 jit_solution(2012601517563739829)
XLA Ops:
  0.0 0.0 copy-start
  0.0 1.0 %copy-done = bf16[128,2048]{1,0:T(8,128)(2,1)S(1)} copy-done((bf16[128,2048]{1,0:T(8,128)(2,1)S(1)}, bf16[128,2048]{1,0:T(8,128)(2,1)}, u32[]{:S(2)}) %copy-start) | copy-done | bytes 524312
  1.0 0.0 copy-start.1
  1.0 0.9 %copy-done.1 = bf16[128,512]{1,0:T(8,128)(2,1)S(1)} copy-done((bf16[128,512]{1,0:T(8,128)(2,1)S(1)}, bf16[128,512]{1,0:T(8,128)(2,1)}, u32[]{:S(2)}) %copy-start.1) | copy-done | bytes 131096
  1.9 0.0 copy-start.2
  1.9 0.9 %copy-done.2 = bf16[128,512]{1,0:T(8,128)(2,1)S(1)} copy-done((bf16[128,512]{1,0:T(8,128)(2,1)S(1)}, bf16[128,512]{1,0:T(8,128)(2,1)}, u32[]{:S(2)}) %copy-start.2) | copy-done | bytes 131096
  2.9 0.0 copy-start.3
  2.9 0.7 %copy-done.3 = s32[4]{0:T(128)S(1)} copy-done((s32[4]{0:T(128)S(1)}, s32[4]{0:T(128)}, u32[]{:S(2)}) %copy-start.3) | copy-done | bytes 40
  3.5 24.7 %relay_attention.1 = bf16[128,2048]{1,0:T(8,128)(2,1)S(1)} custom-call(s32[4]{0:T(128)S(1)} %copy-done.3, bf16[128,2048]{1,0:T(8,128)(2,1)S(1)} %copy-done, bf16[128,512]{1,0:T(8,128)(2,1)S(1)} %copy-done.1, bf16[128,512]{1,0:T(8,128)(2,1)S(1)} %copy-done.2), custom_call_target="tpu_custom_call" | custom-call | flops 1207959552 | bytes 4194304 | tf_op jit(solution)/shard_map/relay_attention/pallas_call | solution.py:409
  28.2 0.8 %copy.6 = bf16[128,2048]{1,0:T(8,128)(2,1)} copy(bf16[128,2048]{1,0:T(8,128)(2,1)S(1)} %relay_attention.1) | data formatting | bytes 1048576
Async XLA Ops:
  0.0 1.0 %copy-start = (bf16[128,2048]{1,0:T(8,128)(2,1)S(1)}, bf16[128,2048]{1,0:T(8,128)(2,1)}, u32[]{:S(2)}) copy-start(bf16[128,2048]{1,0:T(8,128)(2,1)} %q_hbm.1) | copy-start | bytes 1572868
  1.0 0.9 %copy-start.1 = (bf16[128,512]{1,0:T(8,128)(2,1)S(1)}, bf16[128,512]{1,0:T(8,128)(2,1)}, u32[]{:S(2)}) copy-start(bf16[128,512]{1,0:T(8,128)(2,1)} %k_hbm.1) | copy-start | bytes 393220
  1.9 0.9 %copy-start.2 = (bf16[128,512]{1,0:T(8,128)(2,1)S(1)}, bf16[128,512]{1,0:T(8,128)(2,1)}, u32[]{:S(2)}) copy-start(bf16[128,512]{1,0:T(8,128)(2,1)} %v_hbm.1) | copy-start | bytes 393220
  2.9 0.7 %copy-start.3 = (s32[4]{0:T(128)S(1)}, s32[4]{0:T(128)}, u32[]{:S(2)}) copy-start(s32[4]{0:T(128)} %lengths.1) | copy-start | bytes 52

commit v2 on v1

--- a/solution.py
+++ b/solution.py
@@ -105,9 +105,9 @@
 
 
 def relay_kernel(
-    lengths, q_hbm, k_hbm, v_hbm, o_hbm,
-    held, q_rows, q_cols, row_max, row_sum, total, o_rows,
-    own_sem, q_sem, o_sem, send_sem, recv_sem,
+    lengths_hbm, q_hbm, k_hbm, v_hbm, o_hbm,
+    lengths, held, q_rows, q_cols, row_max, row_sum, total, o_rows,
+    lengths_sem, own_sem, q_sem, o_sem, send_sem, recv_sem,
 ):
     tokens = q_hbm.shape[0]
     lanes = GROUP_HEADS * tokens
@@ -146,10 +146,12 @@
         hop(kind, head, here, here, twin).wait_recv()
 
     q_copy = pltpu.make_async_copy(q_hbm, q_rows, q_sem)
+    lengths_copy = pltpu.make_async_copy(lengths_hbm, lengths, lengths_sem)
     for head in range(KEY_VALUE_HEADS):
         for copy in own_copies(head):
             copy.start()
     q_copy.start()
+    lengths_copy.start()
 
     barrier = pltpu.get_barrier_semaphore()
 
@@ -189,10 +191,9 @@
         def _():
             send(Y0, head, 0, y, c, across)
 
-        @pl.when(c == 0)
-        def _():
-            send(C0, head, 0, y, c, twin)
-
+        send(C0, head, 0, y, c, twin)
+
+    lengths_copy.wait()
     q_copy.wait()
     for head in range(QUERY_HEADS):
         rows = q_rows[:, head * HEAD_WIDTH:(head + 1) * HEAD_WIDTH].astype(jnp.float32)
@@ -208,25 +209,20 @@
 
     half = lanes // 2
 
-    def attend(head, behind, from_y, from_c, pair, own=False):
-        if pair:
-            keys = held[behind, head, from_y, 0].reshape(2 * tokens, HEAD_WIDTH)
-            values = held[behind, head, from_y, 1].reshape(2 * tokens, HEAD_WIDTH)
-        else:
-            keys = held[behind, head, from_y, 0, from_c]
-            values = held[behind, head, from_y, 1, from_c]
-        count = keys.shape[0]
-        key_start = ((z - behind) * 4 + from_y * 2 + (0 if pair else from_c)) * tokens
-        key_pos = key_start + lax.broadcasted_iota(jnp.int32, (count, half), 0)
+    def attend(head, behind, from_y, first=False):
+        keys = held[behind, head, from_y, 0].reshape(2 * tokens, HEAD_WIDTH)
+        values = held[behind, head, from_y, 1].reshape(2 * tokens, HEAD_WIDTH)
+        key_start = ((z - behind) * 4 + from_y * 2) * tokens
+        key_pos = key_start + lax.broadcasted_iota(jnp.int32, (2 * tokens, half), 0)
         for part in range(2):
             cols = slice(part * half, (part + 1) * half)
             scores = jnp.dot(keys, q_cols[head, :, cols], preferred_element_type=jnp.float32)
             allowed = key_pos >= query_start[:, cols]
-            if own:
+            if first:
                 allowed = allowed & (key_pos <= query_pos[:, cols])
             scores = jnp.where(allowed, scores, masked_score)
             new_max = jnp.max(scores, axis=0, keepdims=True)
-            if not own:
+            if not first:
                 old_max = row_max[head, :, cols]
                 new_max = jnp.maximum(old_max, new_max)
             weights = jnp.exp2((scores - new_max) * EXP2_SCALE)
@@ -235,7 +231,7 @@
                 values, weights.astype(jnp.bfloat16), (((0,), (0,)), ((), ())),
                 preferred_element_type=jnp.float32,
             )
-            if own:
+            if first:
                 row_sum[head, :, cols] = weight_sum
                 total[head, :, cols] = mixed
             else:
@@ -244,10 +240,6 @@
                 total[head, :, cols] = total[head, :, cols] * factor + mixed
             row_max[head, :, cols] = new_max
 
-    @pl.loop(0, KEY_VALUE_HEADS)
-    def _(head):
-        attend(head, 0, y, c, False, own=True)
-
     @pl.loop(0, KEY_VALUE_HEADS + 1)
     def _(step):
         @pl.when(step < KEY_VALUE_HEADS)
@@ -268,26 +260,30 @@
                 arrived(Y0, step, 0, 0, c)
                 send(C0Y, step, 0, 0, c, twin)
 
+            arrived(C0, step, 0, y, 1 - c)
+            attend(step, 0, y, first=True)
+
         @pl.when(step >= 1)
         def _():
             head = step - 1
 
-            @pl.when(c == 1)
-            def _():
-                arrived(C0, head, 0, y, 0)
-                attend(head, 0, y, 0, False)
-
             @pl.when(y == 1)
             def _():
                 arrived(C0Y, head, 0, 0, 1 - c)
-                attend(head, 0, 0, 0, True)
+                attend(head, 0, 0)
 
             @pl.when(z >= 1)
             def _():
                 arrived(C1, head, 1, y, 1 - c)
-                attend(head, 1, y, 0, True)
-
-    @pl.loop(0, KEY_VALUE_HEADS + 1)
+                attend(head, 1, y)
+
+    def o_copy(head):
+        columns = pl.ds(pl.multiple_of(head * lanes, lanes), lanes)
+        return pltpu.make_async_copy(o_rows.at[head], o_hbm.at[:, columns], o_sem.at[head])
+
+    from_across = (z >= 2) & (y == 0)
+
+    @pl.loop(0, KEY_VALUE_HEADS + 2)
     def _(step):
         @pl.when(step < KEY_VALUE_HEADS)
         def _():
@@ -304,49 +300,35 @@
                 def _():
                     send(Y2, step, 2, y, c, across)
 
-                @pl.when(c == 1)
-                def _():
-                    send(C2, step, 2, y, c, twin)
-
-        @pl.when(step >= 1)
+                send(C2, step, 2, y, c, twin)
+
+        @pl.when((step >= 1) & (step <= KEY_VALUE_HEADS))
         def _():
             head = step - 1
 
             @pl.when(z >= 1)
             def _():
                 arrived(C1Y, head, 1, 1 - y, 1 - c)
-                attend(head, 1, 1 - y, 0, True)
+                attend(head, 1, 1 - y)
 
             @pl.when(z >= 2)
             def _():
-                attend(head, 2, y, c, False)
-
-                @pl.when(c == 0)
-                def _():
-                    arrived(C2, head, 2, y, 1)
-                    attend(head, 2, y, 1, False)
-
-    def o_copy(head):
-        columns = pl.ds(pl.multiple_of(head * lanes, lanes), lanes)
-        return pltpu.make_async_copy(o_rows.at[head], o_hbm.at[:, columns], o_sem.at[head])
-
-    from_across = (z >= 2) & (y == 0)
-
-    @pl.loop(0, KEY_VALUE_HEADS + 1)
-    def _(step):
-        @pl.when((step < KEY_VALUE_HEADS) & from_across)
-        def _():
-            arrived(Y2, step, 2, 1, c)
-            send(C2Y, step, 2, 1, c, twin)
-
-        @pl.when(step >= 1)
-        def _():
-            head = step - 1
+                arrived(C2, head, 2, y, 1 - c)
+                attend(head, 2, y)
 
             @pl.when(from_across)
             def _():
+                arrived(Y2, head, 2, 1, c)
+                send(C2Y, head, 2, 1, c, twin)
+
+        @pl.when(step >= 2)
+        def _():
+            head = step - 2
+
+            @pl.when(from_across)
+            def _():
                 arrived(C2Y, head, 2, 1, 1 - c)
-                attend(head, 2, 1, 0, True)
+                attend(head, 2, 1)
 
             result = total[head] / row_sum[head]
             for at in range(GROUP_HEADS):
@@ -370,9 +352,7 @@
         def _():
             sent(Y0, 0, y, c)
 
-        @pl.when(c == 0)
-        def _():
-            sent(C0, 0, y, c)
+        sent(C0, 0, y, c)
 
         @pl.when(y == 1)
         def _():
@@ -392,7 +372,7 @@
         def _():
             sent(Y2, 2, y, c)
 
-        @pl.when((z >= 2) & (c == 1))
+        @pl.when(z >= 2)
         def _():
             sent(C2, 2, y, c)
 
@@ -404,14 +384,15 @@
 def relay_attention(rotated_queries, key_rows, value_matrix, doc_lengths):
     tokens = rotated_queries.shape[0]
     lanes = GROUP_HEADS * tokens
-    anywhere = pl.BlockSpec(memory_space=pl.ANY)
+    in_hbm = pl.BlockSpec(memory_space=pltpu.HBM)
     pairs = 9 * tokens * tokens * QUERY_HEADS
     return pl.pallas_call(
         relay_kernel,
         out_shape=jax.ShapeDtypeStruct(rotated_queries.shape, jnp.bfloat16),
-        in_specs=[pl.BlockSpec(memory_space=pltpu.SMEM), anywhere, anywhere, anywhere],
-        out_specs=anywhere,
+        in_specs=[in_hbm] * 4,
+        out_specs=pl.BlockSpec(memory_space=pl.ANY),
         scratch_shapes=[
+            pltpu.SMEM(doc_lengths.shape, jnp.int32),
             pltpu.VMEM((3, KEY_VALUE_HEADS, 2, 2, 2, tokens, HEAD_WIDTH), jnp.bfloat16),
             pltpu.VMEM(rotated_queries.shape, jnp.bfloat16),
             pltpu.VMEM((KEY_VALUE_HEADS, HEAD_WIDTH, lanes), jnp.bfloat16),
@@ -419,6 +400,7 @@
             pltpu.VMEM((KEY_VALUE_HEADS, 1, lanes), jnp.float32),
             pltpu.VMEM((KEY_VALUE_HEADS, HEAD_WIDTH, lanes), jnp.float32),
             pltpu.VMEM((KEY_VALUE_HEADS, tokens, GROUP_HEADS * HEAD_WIDTH), jnp.bfloat16),
+            pltpu.SemaphoreType.DMA,
             pltpu.SemaphoreType.DMA((2, KEY_VALUE_HEADS)),
             pltpu.SemaphoreType.DMA,
             pltpu.SemaphoreType.DMA((KEY_VALUE_HEADS,)),

time: 29.2 us -> 31.7 us (1.086)
  Pallas kernels: 24.7 us -> 27.2 us
    pallas_call x1, Pallas kernels: 24.7 us -> 27.2 us  [relay_attention(): pl.pallas_call(relay_kernel, out_shape=jax.ShapeDtypeStruct(rotated_queri...]
where the time goes in v2:
time: 31.7 us; the launch traced here: 31.5 us
  Pallas kernels  27.2 us (86%)
  local copies, waits for them, and re-layouts  4.3 us (14%)
    pallas_call x1, Pallas kernels, relay_attention(): pl.pallas_call(relay_kernel, out_shape=jax.ShapeDtypeStruct(rotated_queri...  27.2 us
    unnamed x9, local copies, waits for them, and re-layouts  4.3 us

profile of v2, /device:TPU:17, one launch (start us, length us, event | category | flops | bytes accessed | tf_op | source)
XLA Modules:
  0.0 31.5 jit_solution(14192475253391991791)
XLA Ops:
  0.0 0.0 copy-start
  0.0 1.0 %copy-done = bf16[128,2048]{1,0:T(8,128)(2,1)S(1)} copy-done((bf16[128,2048]{1,0:T(8,128)(2,1)S(1)}, bf16[128,2048]{1,0:T(8,128)(2,1)}, u32[]{:S(2)}) %copy-start) | copy-done | bytes 524312
  1.0 0.0 copy-start.1
  1.0 0.9 %copy-done.1 = bf16[128,512]{1,0:T(8,128)(2,1)S(1)} copy-done((bf16[128,512]{1,0:T(8,128)(2,1)S(1)}, bf16[128,512]{1,0:T(8,128)(2,1)}, u32[]{:S(2)}) %copy-start.1) | copy-done | bytes 131096
  1.9 0.0 copy-start.2
  1.9 0.9 %copy-done.2 = bf16[128,512]{1,0:T(8,128)(2,1)S(1)} copy-done((bf16[128,512]{1,0:T(8,128)(2,1)S(1)}, bf16[128,512]{1,0:T(8,128)(2,1)}, u32[]{:S(2)}) %copy-start.2) | copy-done | bytes 131096
  2.9 0.0 copy-start.3
  2.9 0.7 %copy-done.3 = s32[4]{0:T(128)S(1)} copy-done((s32[4]{0:T(128)S(1)}, s32[4]{0:T(128)}, u32[]{:S(2)}) %copy-start.3) | copy-done | bytes 40
  3.5 27.2 %relay_attention.1 = bf16[128,2048]{1,0:T(8,128)(2,1)S(1)} custom-call(s32[4]{0:T(128)S(1)} %copy-done.3, bf16[128,2048]{1,0:T(8,128)(2,1)S(1)} %copy-done, bf16[128,512]{1,0:T(8,128)(2,1)S(1)} %copy-done.1, bf16[128,512]{1,0:T(8,128)(2,1)S(1)} %copy-done.2), custom_call_target="tpu_custom_call" | custom-call | flops 1207959552 | bytes 4194304 | tf_op jit(solution)/shard_map/relay_attention/pallas_call | solution.py:389
  30.7 0.8 %copy.6 = bf16[128,2048]{1,0:T(8,128)(2,1)} copy(bf16[128,2048]{1,0:T(8,128)(2,1)S(1)} %relay_attention.1) | data formatting | bytes 1048576
Async XLA Ops:
  0.0 1.0 %copy-start = (bf16[128,2048]{1,0:T(8,128)(2,1)S(1)}, bf16[128,2048]{1,0:T(8,128)(2,1)}, u32[]{:S(2)}) copy-start(bf16[128,2048]{1,0:T(8,128)(2,1)} %q_hbm.1) | copy-start | bytes 1572868
  1.0 0.9 %copy-start.1 = (bf16[128,512]{1,0:T(8,128)(2,1)S(1)}, bf16[128,512]{1,0:T(8,128)(2,1)}, u32[]{:S(2)}) copy-start(bf16[128,512]{1,0:T(8,128)(2,1)} %k_hbm.1) | copy-start | bytes 393220
  1.9 0.9 %copy-start.2 = (bf16[128,512]{1,0:T(8,128)(2,1)S(1)}, bf16[128,512]{1,0:T(8,128)(2,1)}, u32[]{:S(2)}) copy-start(bf16[128,512]{1,0:T(8,128)(2,1)} %v_hbm.1) | copy-start | bytes 393220
  2.9 0.7 %copy-start.3 = (s32[4]{0:T(128)S(1)}, s32[4]{0:T(128)}, u32[]{:S(2)}) copy-start(s32[4]{0:T(128)} %lengths_hbm.1) | copy-start | bytes 52

commit v3 on v2

--- a/solution.py
+++ b/solution.py
@@ -102,12 +102,13 @@
 
 (Z1, Z2, C0, Y0, C0Y, C1, Y1, C1Y, C2, Y2, C2Y) = range(11)
 HOPS = 11
+HEADS_AT_ONCE = 2
 
 
 def relay_kernel(
     lengths_hbm, q_hbm, k_hbm, v_hbm, o_hbm,
-    lengths, held, q_rows, q_cols, row_max, row_sum, total, o_rows,
-    lengths_sem, own_sem, q_sem, o_sem, send_sem, recv_sem,
+    lengths, held, q_rows, v_rows, q_cols, row_max, row_sum, total, o_rows,
+    lengths_sem, k_sem, v_sem, q_sem, o_sem, send_sem, recv_sem,
 ):
     tokens = q_hbm.shape[0]
     lanes = GROUP_HEADS * tokens
@@ -124,12 +125,13 @@
     def slot(behind, head, from_y, from_c):
         return held.at[behind, head, from_y, :, from_c]
 
-    def own_copies(head):
+    def k_copy(head):
         columns = pl.ds(head * HEAD_WIDTH, HEAD_WIDTH)
-        return [
-            pltpu.make_async_copy(source.at[:, columns], held.at[0, head, y, which, c], own_sem.at[which, head])
-            for which, source in enumerate((k_hbm, v_hbm))
-        ]
+        return pltpu.make_async_copy(k_hbm.at[:, columns], held.at[0, head, y, 0, c], k_sem.at[head])
+
+    def v_copy(head):
+        columns = pl.ds(head * HEAD_WIDTH, HEAD_WIDTH)
+        return pltpu.make_async_copy(v_hbm.at[:, columns], v_rows.at[head], v_sem.at[head])
 
     def hop(kind, head, source, target, device):
         return pltpu.make_async_remote_copy(
@@ -148,8 +150,8 @@
     q_copy = pltpu.make_async_copy(q_hbm, q_rows, q_sem)
     lengths_copy = pltpu.make_async_copy(lengths_hbm, lengths, lengths_sem)
     for head in range(KEY_VALUE_HEADS):
-        for copy in own_copies(head):
-            copy.start()
+        v_copy(head).start()
+        k_copy(head).start()
     q_copy.start()
     lengths_copy.start()
 
@@ -169,6 +171,10 @@
     def _():
         greet(down)
 
+    for head in range(KEY_VALUE_HEADS):
+        v_copy(head).wait()
+        held[0, head, y, 1, c] = v_rows[head].astype(jnp.float32).T.astype(jnp.bfloat16)
+
     inner = (z > 0) & (z < 3)
 
     @pl.when(inner)
@@ -180,8 +186,7 @@
         pl.semaphore_wait(barrier, 3)
 
     for head in range(KEY_VALUE_HEADS):
-        for copy in own_copies(head):
-            copy.wait()
+        k_copy(head).wait()
 
         @pl.when(z < 3)
         def _():
@@ -191,7 +196,9 @@
         def _():
             send(Y0, head, 0, y, c, across)
 
-        send(C0, head, 0, y, c, twin)
+        @pl.when(c == 0)
+        def _():
+            send(C0, head, 0, y, c, twin)
 
     lengths_copy.wait()
     q_copy.wait()
@@ -208,18 +215,36 @@
         query_start = query_start + jnp.where(doc_end <= query_pos, lengths[doc], 0)
 
     half = lanes // 2
-
-    def attend(head, behind, from_y, first=False):
-        keys = held[behind, head, from_y, 0].reshape(2 * tokens, HEAD_WIDTH)
-        values = held[behind, head, from_y, 1].reshape(2 * tokens, HEAD_WIDTH)
-        key_start = ((z - behind) * 4 + from_y * 2) * tokens
-        key_pos = key_start + lax.broadcasted_iota(jnp.int32, (2 * tokens, half), 0)
-        for part in range(2):
-            cols = slice(part * half, (part + 1) * half)
-            scores = jnp.dot(keys, q_cols[head, :, cols], preferred_element_type=jnp.float32)
-            allowed = key_pos >= query_start[:, cols]
+    chains = [(at, part) for at in range(HEADS_AT_ONCE) for part in range(2)]
+
+    def attend(heads, behind, from_y, from_c, first=False):
+        count = tokens if from_c is not None else 2 * tokens
+        key_start = ((z - behind) * 4 + from_y * 2 + (0 if from_c is None else from_c)) * tokens
+        key_pos = lax.broadcasted_iota(jnp.int32, (count, half), 0)
+
+        def cols_of(part):
+            return slice(part * half, (part + 1) * half)
+
+        def scores_of(chain):
+            at, part = chain
+            if from_c is None:
+                keys = held[behind, heads + at, from_y, 0].reshape(count, HEAD_WIDTH)
+            else:
+                keys = held[behind, heads + at, from_y, 0, from_c]
+            return jnp.dot(keys, q_cols[heads + at, :, cols_of(part)], preferred_element_type=jnp.float32)
+
+        def fold(chain, scores):
+            at, part = chain
+            head, cols = heads + at, cols_of(part)
+            if from_c is None:
+                values = jnp.concatenate(
+                    [held[behind, head, from_y, 1, 0], held[behind, head, from_y, 1, 1]], axis=1
+                )
+            else:
+                values = held[behind, head, from_y, 1, from_c]
+            allowed = key_pos >= query_start[:, cols] - key_start
             if first:
-                allowed = allowed & (key_pos <= query_pos[:, cols])
+                allowed = allowed & (key_pos <= query_pos[:, cols] - key_start)
             scores = jnp.where(allowed, scores, masked_score)
             new_max = jnp.max(scores, axis=0, keepdims=True)
             if not first:
@@ -227,10 +252,7 @@
                 new_max = jnp.maximum(old_max, new_max)
             weights = jnp.exp2((scores - new_max) * EXP2_SCALE)
             weight_sum = jnp.sum(weights, axis=0, keepdims=True)
-            mixed = lax.dot_general(
-                values, weights.astype(jnp.bfloat16), (((0,), (0,)), ((), ())),
-                preferred_element_type=jnp.float32,
-            )
+            mixed = jnp.dot(values, weights.astype(jnp.bfloat16), preferred_element_type=jnp.float32)
             if first:
                 row_sum[head, :, cols] = weight_sum
                 total[head, :, cols] = mixed
@@ -240,42 +262,70 @@
                 total[head, :, cols] = total[head, :, cols] * factor + mixed
             row_max[head, :, cols] = new_max
 
-    @pl.loop(0, KEY_VALUE_HEADS + 1)
+        ready = scores_of(chains[0])
+        for number, chain in enumerate(chains):
+            scores = ready
+            if number + 1 < len(chains):
+                ready = scores_of(chains[number + 1])
+            fold(chain, scores)
+
+    def each(heads, wait):
+        for at in range(HEADS_AT_ONCE):
+            wait(heads + at)
+
+    def pass_on_first(head):
+        @pl.when(z >= 1)
+        def _():
+            arrived(Z1, head, 1, y, c)
+
+            @pl.when(z < 3)
+            def _():
+                send(Z2, head, 1, y, c, up, landing=2)
+
+            send(Y1, head, 1, y, c, across)
+            send(C1, head, 1, y, c, twin)
+
+        @pl.when(y == 1)
+        def _():
+            arrived(Y0, head, 0, 0, c)
+            send(C0Y, head, 0, 0, c, twin)
+
+    steps = KEY_VALUE_HEADS // HEADS_AT_ONCE
+
+    @pl.loop(0, steps + 1)
     def _(step):
-        @pl.when(step < KEY_VALUE_HEADS)
-        def _():
+        @pl.when(step < steps)
+        def _():
+            pass_on_first(step * HEADS_AT_ONCE)
+
+        @pl.when(step >= 1)
+        def _():
+            heads = (step - 1) * HEADS_AT_ONCE
+
+            @pl.when(y == 1)
+            def _():
+                each(heads, lambda head: arrived(C0Y, head, 0, 0, 1 - c))
+                attend(heads, 0, 0, None)
+
             @pl.when(z >= 1)
             def _():
-                arrived(Z1, step, 1, y, c)
-
-                @pl.when(z < 3)
-                def _():
-                    send(Z2, step, 1, y, c, up, landing=2)
-
-                send(Y1, step, 1, y, c, across)
-                send(C1, step, 1, y, c, twin)
-
-            @pl.when(y == 1)
-            def _():
-                arrived(Y0, step, 0, 0, c)
-                send(C0Y, step, 0, 0, c, twin)
-
-            arrived(C0, step, 0, y, 1 - c)
-            attend(step, 0, y, first=True)
-
-        @pl.when(step >= 1)
-        def _():
-            head = step - 1
-
-            @pl.when(y == 1)
-            def _():
-                arrived(C0Y, head, 0, 0, 1 - c)
-                attend(head, 0, 0)
-
-            @pl.when(z >= 1)
-            def _():
-                arrived(C1, head, 1, y, 1 - c)
-                attend(head, 1, y)
+                each(heads, lambda head: arrived(C1, head, 1, y, 1 - c))
+                attend(heads, 1, y, None)
+
+        @pl.when(step < steps)
+        def _():
+            heads = step * HEADS_AT_ONCE
+            for at in range(1, HEADS_AT_ONCE):
+                pass_on_first(heads + at)
+
+            @pl.when(c == 0)
+            def _():
+                attend(heads, 0, y, 0, first=True)
+
+            @pl.when(c == 1)
+            def _():
+                each(heads, lambda head: arrived(C0, head, 0, y, 0))
+                attend(heads, 0, y, None, first=True)
 
     def o_copy(head):
         columns = pl.ds(pl.multiple_of(head * lanes, lanes), lanes)
@@ -283,58 +333,78 @@
 
     from_across = (z >= 2) & (y == 0)
 
-    @pl.loop(0, KEY_VALUE_HEADS + 2)
+    def pass_on_second(head):
+        @pl.when(z >= 1)
+        def _():
+            arrived(Y1, head, 1, 1 - y, c)
+            send(C1Y, head, 1, 1 - y, c, twin)
+
+        @pl.when(z >= 2)
+        def _():
+            arrived(Z2, head, 2, y, c)
+
+            @pl.when(y == 1)
+            def _():
+                send(Y2, head, 2, y, c, across)
+
+            @pl.when(c == 1)
+            def _():
+                send(C2, head, 2, y, c, twin)
+
+    def pass_on_last(head):
+        arrived(Y2, head, 2, 1, c)
+        send(C2Y, head, 2, 1, c, twin)
+
+    @pl.loop(0, steps + 2)
     def _(step):
-        @pl.when(step < KEY_VALUE_HEADS)
-        def _():
+        @pl.when(step < steps)
+        def _():
+            pass_on_second(step * HEADS_AT_ONCE)
+
+        @pl.when((step >= 1) & (step <= steps))
+        def _():
+            heads = (step - 1) * HEADS_AT_ONCE
+
             @pl.when(z >= 1)
             def _():
-                arrived(Y1, step, 1, 1 - y, c)
-                send(C1Y, step, 1, 1 - y, c, twin)
-
-            @pl.when(z >= 2)
-            def _():
-                arrived(Z2, step, 2, y, c)
-
-                @pl.when(y == 1)
-                def _():
-                    send(Y2, step, 2, y, c, across)
-
-                send(C2, step, 2, y, c, twin)
-
-        @pl.when((step >= 1) & (step <= KEY_VALUE_HEADS))
-        def _():
-            head = step - 1
-
-            @pl.when(z >= 1)
-            def _():
-                arrived(C1Y, head, 1, 1 - y, 1 - c)
-                attend(head, 1, 1 - y)
-
-            @pl.when(z >= 2)
-            def _():
-                arrived(C2, head, 2, y, 1 - c)
-                attend(head, 2, y)
+                each(heads, lambda head: arrived(C1Y, head, 1, 1 - y, 1 - c))
+                attend(heads, 1, 1 - y, None)
+
+            @pl.when((z >= 2) & (c == 0))
+            def _():
+                each(heads, lambda head: arrived(C2, head, 2, y, 1))
+                attend(heads, 2, y, None)
+
+            @pl.when((z >= 2) & (c == 1))
+            def _():
+                attend(heads, 2, y, 1)
+
+        @pl.when(step < steps)
+        def _():
+            for at in range(1, HEADS_AT_ONCE):
+                pass_on_second(step * HEADS_AT_ONCE + at)
+
+        @pl.when(step >= 2)
+        def _():
+            heads = (step - 2) * HEADS_AT_ONCE
 
             @pl.when(from_across)
             def _():
-                arrived(Y2, head, 2, 1, c)
-                send(C2Y, head, 2, 1, c, twin)
-
-        @pl.when(step >= 2)
-        def _():
-            head = step - 2
-
-            @pl.when(from_across)
-            def _():
-                arrived(C2Y, head, 2, 1, 1 - c)
-                attend(head, 2, 1)
-
-            result = total[head] / row_sum[head]
-            for at in range(GROUP_HEADS):
-                own_cols = slice(at * tokens, (at + 1) * tokens)
-                o_rows[head, :, at * HEAD_WIDTH:(at + 1) * HEAD_WIDTH] = result[:, own_cols].T.astype(jnp.bfloat16)
-            o_copy(head).start()
+                each(heads, lambda head: arrived(C2Y, head, 2, 1, 1 - c))
+                attend(heads, 2, 1, None)
+
+            for at in range(HEADS_AT_ONCE):
+                head = heads + at
+                result = total[head] * (1.0 / row_sum[head])
+                for own in range(GROUP_HEADS):
+                    own_cols = slice(own * tokens, (own + 1) * tokens)
+                    columns = slice(own * HEAD_WIDTH, (own + 1) * HEAD_WIDTH)
+                    o_rows[head, :, columns] = result[:, own_cols].T.astype(jnp.bfloat16)
+                o_copy(head).start()
+
+        @pl.when((step >= 1) & (step <= steps) & from_across)
+        def _():
+            each((step - 1) * HEADS_AT_ONCE, pass_on_last)
 
     @pl.loop(0, KEY_VALUE_HEADS)
     def _(head):
@@ -352,7 +422,9 @@
         def _():
             sent(Y0, 0, y, c)
 
-        sent(C0, 0, y, c)
+        @pl.when(c == 0)
+        def _():
+            sent(C0, 0, y, c)
 
         @pl.when(y == 1)
         def _():
@@ -372,7 +444,7 @@
         def _():
             sent(Y2, 2, y, c)
 
-        @pl.when(z >= 2)
+        @pl.when((z >= 2) & (c == 1))
         def _():
             sent(C2, 2, y, c)
 
@@ -384,7 +456,7 @@
 def relay_attention(rotated_queries, key_rows, value_matrix, doc_lengths):
     tokens = rotated_queries.shape[0]
     lanes = GROUP_HEADS * tokens
-    in_hbm = pl.BlockSpec(memory_space=pltpu.HBM)
+    in_hbm = pl.BlockSpec(memory_space=pl.ANY)
     pairs = 9 * tokens * tokens * QUERY_HEADS
     return pl.pallas_call(
         relay_kernel,
@@ -395,20 +467,22 @@
             pltpu.SMEM(doc_lengths.shape, jnp.int32),
             pltpu.VMEM((3, KEY_VALUE_HEADS, 2, 2, 2, tokens, HEAD_WIDTH), jnp.bfloat16),
             pltpu.VMEM(rotated_queries.shape, jnp.bfloat16),
+            pltpu.VMEM((KEY_VALUE_HEADS, tokens, HEAD_WIDTH), jnp.bfloat16),
             pltpu.VMEM((KEY_VALUE_HEADS, HEAD_WIDTH, lanes), jnp.bfloat16),
             pltpu.VMEM((KEY_VALUE_HEADS, 1, lanes), jnp.float32),
             pltpu.VMEM((KEY_VALUE_HEADS, 1, lanes), jnp.float32),
             pltpu.VMEM((KEY_VALUE_HEADS, HEAD_WIDTH, lanes), jnp.float32),
             pltpu.VMEM((KEY_VALUE_HEADS, tokens, GROUP_HEADS * HEAD_WIDTH), jnp.bfloat16),
             pltpu.SemaphoreType.DMA,
-            pltpu.SemaphoreType.DMA((2, KEY_VALUE_HEADS)),
+            pltpu.SemaphoreType.DMA((KEY_VALUE_HEADS,)),
+            pltpu.SemaphoreType.DMA((KEY_VALUE_HEADS,)),
             pltpu.SemaphoreType.DMA,
             pltpu.SemaphoreType.DMA((KEY_VALUE_HEADS,)),
             pltpu.SemaphoreType.DMA((HOPS, KEY_VALUE_HEADS)),
             pltpu.SemaphoreType.DMA((HOPS, KEY_VALUE_HEADS)),
         ],
         compiler_params=pltpu.CompilerParams(
-            collective_id=0, has_side_effects=True, vmem_limit_bytes=32 * 1024 * 1024
+            collective_id=0, has_side_effects=True, vmem_limit_bytes=64 * 1024 * 1024
         ),
         cost_estimate=pl.CostEstimate(
             flops=4 * pairs * HEAD_WIDTH, bytes_accessed=4 * 1024 * 1024, transcendentals=pairs

time: 31.7 us -> 26.9 us (0.85)
  local copies, waits for them, and re-layouts: 4.3 us -> 1.88 us
  Pallas kernels: 27.2 us -> 24.8 us
    unnamed x9 -> x1, local copies, waits for them, and re-layouts: 4.3 us -> 1.88 us
    pallas_call x1, Pallas kernels: 27.2 us -> 24.8 us  [relay_attention(): pl.pallas_call(relay_kernel, out_shape=jax.ShapeDtypeStruct(rotated_queri...]
where the time goes in v3:
time: 26.9 us; the launch traced here: 26.7 us
  Pallas kernels  24.8 us (92%)
  local copies, waits for them, and re-layouts  1.88 us (7%)
    pallas_call x1, Pallas kernels, relay_attention(): pl.pallas_call(relay_kernel, out_shape=jax.ShapeDtypeStruct(rotated_queri...  24.8 us
    unnamed x1, local copies, waits for them, and re-layouts  1.88 us

profile of v3, /device:TPU:17, one launch (start us, length us, event | category | flops | bytes accessed | tf_op | source)
XLA Modules:
  0.0 26.7 jit_solution(10081187887511476641)
XLA Ops:
  0.0 24.8 %relay_attention.1 = bf16[128,2048]{1,0:T(8,128)(2,1)} custom-call(s32[4]{0:T(128)} %lengths_hbm.1, bf16[128,2048]{1,0:T(8,128)(2,1)} %q_hbm.1, bf16[128,512]{1,0:T(8,128)(2,1)} %k_hbm.1, bf16[128,512]{1,0:T(8,128)(2,1)} %v_hbm.1), custom_call_target="tpu_custom_call" | custom-call | flops 1207959552 | bytes 4194304 | tf_op jit(solution)/shard_map/relay_attention/pallas_call | solution.py:461
  24.8 1.9 %copy.6 = bf16[128,2048]{1,0:T(8,128)(2,1)} copy(bf16[128,2048]{1,0:T(8,128)(2,1)} %relay_attention.1) | data formatting | bytes 1048576

commit v4 on v3

--- a/solution.py
+++ b/solution.py
@@ -100,8 +100,8 @@
 GROUP_HEADS = QUERY_HEADS // KEY_VALUE_HEADS
 EXP2_SCALE = math.log2(math.e) / math.sqrt(HEAD_WIDTH)
 
-(Z1, Z2, C0, Y0, C0Y, C1, Y1, C1Y, C2, Y2, C2Y) = range(11)
-HOPS = 11
+(Z1, Z2, C0, C1, C2, YA, YB, CYA, CYB) = range(9)
+HOPS = 9
 HEADS_AT_ONCE = 2
 
 
@@ -194,7 +194,7 @@
 
         @pl.when(y == 0)
         def _():
-            send(Y0, head, 0, y, c, across)
+            send(YA, head, 0, y, c, across)
 
         @pl.when(c == 0)
         def _():
@@ -273,7 +273,7 @@
         for at in range(HEADS_AT_ONCE):
             wait(heads + at)
 
-    def pass_on_first(head):
+    def z_first(head):
         @pl.when(z >= 1)
         def _():
             arrived(Z1, head, 1, y, c)
@@ -282,129 +282,129 @@
             def _():
                 send(Z2, head, 1, y, c, up, landing=2)
 
-            send(Y1, head, 1, y, c, across)
+            send(YB - y, head, 1, y, c, across)
             send(C1, head, 1, y, c, twin)
 
-        @pl.when(y == 1)
-        def _():
-            arrived(Y0, head, 0, 0, c)
-            send(C0Y, head, 0, 0, c, twin)
-
-    steps = KEY_VALUE_HEADS // HEADS_AT_ONCE
-
-    @pl.loop(0, steps + 1)
-    def _(step):
-        @pl.when(step < steps)
-        def _():
-            pass_on_first(step * HEADS_AT_ONCE)
-
-        @pl.when(step >= 1)
-        def _():
-            heads = (step - 1) * HEADS_AT_ONCE
+    def z_second(head):
+        @pl.when(z >= 2)
+        def _():
+            arrived(Z2, head, 2, y, c)
 
             @pl.when(y == 1)
             def _():
-                each(heads, lambda head: arrived(C0Y, head, 0, 0, 1 - c))
-                attend(heads, 0, 0, None)
-
-            @pl.when(z >= 1)
-            def _():
-                each(heads, lambda head: arrived(C1, head, 1, y, 1 - c))
-                attend(heads, 1, y, None)
-
-        @pl.when(step < steps)
-        def _():
-            heads = step * HEADS_AT_ONCE
-            for at in range(1, HEADS_AT_ONCE):
-                pass_on_first(heads + at)
-
-            @pl.when(c == 0)
-            def _():
-                attend(heads, 0, y, 0, first=True)
+                send(YB, head, 2, y, c, across)
 
             @pl.when(c == 1)
             def _():
-                each(heads, lambda head: arrived(C0, head, 0, y, 0))
-                attend(heads, 0, y, None, first=True)
+                send(C2, head, 2, y, c, twin)
+
+    crosses_first, crosses_second = z + y >= 1, z + y >= 2
+
+    def y_first(head):
+        @pl.when(crosses_first)
+        def _():
+            arrived(YA, head, 1 - y, 1 - y, c)
+            send(CYA, head, 1 - y, 1 - y, c, twin)
+
+    def y_second(head):
+        @pl.when(crosses_second)
+        def _():
+            arrived(YB, head, 2 - y, 1 - y, c)
+            send(CYB, head, 2 - y, 1 - y, c, twin)
 
     def o_copy(head):
         columns = pl.ds(pl.multiple_of(head * lanes, lanes), lanes)
         return pltpu.make_async_copy(o_rows.at[head], o_hbm.at[:, columns], o_sem.at[head])
 
-    from_across = (z >= 2) & (y == 0)
-
-    def pass_on_second(head):
+    @pl.loop(0, 2)
+    def _(step):
+        heads = step * HEADS_AT_ONCE
+
+        @pl.when(c == 0)
+        def _():
+            attend(heads, 0, y, 0, first=True)
+
+        @pl.when(c == 1)
+        def _():
+            each(heads, lambda head: arrived(C0, head, 0, y, 0))
+            attend(heads, 0, y, None, first=True)
+
+        z_first(step)
+
+    y_first(0)
+
+    @pl.loop(0, 2)
+    def _(step):
+        heads = step * HEADS_AT_ONCE
+
+        @pl.when(step == 0)
+        def _():
+            z_first(2)
+            y_first(1)
+
+        @pl.when(step == 1)
+        def _():
+            y_first(3)
+
         @pl.when(z >= 1)
         def _():
-            arrived(Y1, head, 1, 1 - y, c)
-            send(C1Y, head, 1, 1 - y, c, twin)
-
-        @pl.when(z >= 2)
-        def _():
-            arrived(Z2, head, 2, y, c)
-
-            @pl.when(y == 1)
-            def _():
-                send(Y2, head, 2, y, c, across)
-
-            @pl.when(c == 1)
-            def _():
-                send(C2, head, 2, y, c, twin)
-
-    def pass_on_last(head):
-        arrived(Y2, head, 2, 1, c)
-        send(C2Y, head, 2, 1, c, twin)
-
-    @pl.loop(0, steps + 2)
+            each(heads, lambda head: arrived(C1, head, 1, y, 1 - c))
+            attend(heads, 1, y, None)
+
+        @pl.when(step == 0)
+        def _():
+            z_first(3)
+            y_first(2)
+
+        @pl.when(step == 1)
+        def _():
+            z_second(0)
+
+        @pl.when(crosses_first)
+        def _():
+            each(heads, lambda head: arrived(CYA, head, 1 - y, 1 - y, 1 - c))
+            attend(heads, 1 - y, 1 - y, None)
+
+    z_second(1)
+    y_second(0)
+    z_second(2)
+    y_second(1)
+
+    @pl.loop(0, 2)
     def _(step):
-        @pl.when(step < steps)
-        def _():
-            pass_on_second(step * HEADS_AT_ONCE)
-
-        @pl.when((step >= 1) & (step <= steps))
-        def _():
-            heads = (step - 1) * HEADS_AT_ONCE
-
-            @pl.when(z >= 1)
-            def _():
-                each(heads, lambda head: arrived(C1Y, head, 1, 1 - y, 1 - c))
-                attend(heads, 1, 1 - y, None)
-
-            @pl.when((z >= 2) & (c == 0))
-            def _():
-                each(heads, lambda head: arrived(C2, head, 2, y, 1))
-                attend(heads, 2, y, None)
-
-            @pl.when((z >= 2) & (c == 1))
-            def _():
-                attend(heads, 2, y, 1)
-
-        @pl.when(step < steps)
-        def _():
-            for at in range(1, HEADS_AT_ONCE):
-                pass_on_second(step * HEADS_AT_ONCE + at)
-
-        @pl.when(step >= 2)
-        def _():
-            heads = (step - 2) * HEADS_AT_ONCE
-
-            @pl.when(from_across)
-            def _():
-                each(heads, lambda head: arrived(C2Y, head, 2, 1, 1 - c))
-                attend(heads, 2, 1, None)
-
-            for at in range(HEADS_AT_ONCE):
-                head = heads + at
-                result = total[head] * (1.0 / row_sum[head])
-                for own in range(GROUP_HEADS):
-                    own_cols = slice(own * tokens, (own + 1) * tokens)
-                    columns = slice(own * HEAD_WIDTH, (own + 1) * HEAD_WIDTH)
-                    o_rows[head, :, columns] = result[:, own_cols].T.astype(jnp.bfloat16)
-                o_copy(head).start()
-
-        @pl.when((step >= 1) & (step <= steps) & from_across)
-        def _():
-            each((step - 1) * HEADS_AT_ONCE, pass_on_last)
+        heads = step * HEADS_AT_ONCE
+
+        @pl.when((z >= 2) & (c == 0))
+        def _():
+            each(heads, lambda head: arrived(C2, head, 2, y, 1))
+            attend(heads, 2, y, None)
+
+        @pl.when((z >= 2) & (c == 1))
+        def _():
+            attend(heads, 2, y, 1)
+
+        @pl.when(step == 0)
+        def _():
+            z_second(3)
+            y_second(2)
+
+        @pl.when(step == 1)
+        def _():
+            y_second(3)
+
+        @pl.when(crosses_second)
+        def _():
+            each(heads, lambda head: arrived(CYB, head, 2 - y, 1 - y, 1 - c))
+            attend(heads, 2 - y, 1 - y, None)
+
+        for at in range(HEADS_AT_ONCE):
+            head = heads + at
+            result = total[head] * (1.0 / row_sum[head])
+            for own in range(GROUP_HEADS):
+                own_cols = slice(own * tokens, (own + 1) * tokens)
+                columns = slice(own * HEAD_WIDTH, (own + 1) * HEAD_WIDTH)
+                o_rows[head, :, columns] = result[:, own_cols].T.astype(jnp.bfloat16)
+            o_copy(head).start()
 
     @pl.loop(0, KEY_VALUE_HEADS)
     def _(head):
@@ -418,39 +418,37 @@
         def _():
             sent(Z1, 0, y, c)
 
-        @pl.when(y == 0)
-        def _():
-            sent(Y0, 0, y, c)
-
         @pl.when(c == 0)
         def _():
             sent(C0, 0, y, c)
 
-        @pl.when(y == 1)
-        def _():
-            sent(C0Y, 0, 0, c)
+        @pl.when(z - y >= 0)
+        def _():
+            sent(YA, y, y, c)
+
+        @pl.when(z - y >= 1)
+        def _():
+            sent(YB, 1 + y, y, c)
+
+        @pl.when(crosses_first)
+        def _():
+            sent(CYA, 1 - y, 1 - y, c)
+
+        @pl.when(crosses_second)
+        def _():
+            sent(CYB, 2 - y, 1 - y, c)
 
         @pl.when(z >= 1)
         def _():
+            sent(C1, 1, y, c)
+
             @pl.when(z < 3)
             def _():
                 sent(Z2, 1, y, c)
 
-            sent(Y1, 1, y, c)
-            sent(C1, 1, y, c)
-            sent(C1Y, 1, 1 - y, c)
-
-        @pl.when((z >= 2) & (y == 1))
-        def _():
-            sent(Y2, 2, y, c)
-
         @pl.when((z >= 2) & (c == 1))
         def _():
             sent(C2, 2, y, c)
-
-        @pl.when(from_across)
-        def _():
-            sent(C2Y, 2, 1, c)
 
 
 def relay_attention(rotated_queries, key_rows, value_matrix, doc_lengths):

time: 26.9 us -> 26.1 us (0.970)
  Pallas kernels: 24.8 us -> 24 us
    pallas_call x1, Pallas kernels: 24.8 us -> 24 us  [relay_attention(): pl.pallas_call(relay_kernel, out_shape=jax.ShapeDtypeStruct(rotated_queri...]
where the time goes in v4:
time: 26.1 us; the launch traced here: 25.9 us
  Pallas kernels  24 us (92%)
  local copies, waits for them, and re-layouts  1.88 us (7%)
    pallas_call x1, Pallas kernels, relay_attention(): pl.pallas_call(relay_kernel, out_shape=jax.ShapeDtypeStruct(rotated_queri...  24 us
    unnamed x1, local copies, waits for them, and re-layouts  1.88 us

profile of v4, /device:TPU:17, one launch (start us, length us, event | category | flops | bytes accessed | tf_op | source)
XLA Modules:
  0.0 25.9 jit_solution(10418065083199623534)
XLA Ops:
  0.0 24.0 %relay_attention.1 = bf16[128,2048]{1,0:T(8,128)(2,1)} custom-call(s32[4]{0:T(128)} %lengths_hbm.1, bf16[128,2048]{1,0:T(8,128)(2,1)} %q_hbm.1, bf16[128,512]{1,0:T(8,128)(2,1)} %k_hbm.1, bf16[128,512]{1,0:T(8,128)(2,1)} %v_hbm.1), custom_call_target="tpu_custom_call" | custom-call | flops 1207959552 | bytes 4194304 | tf_op jit(solution)/shard_map/relay_attention/pallas_call | solution.py:459
  24.0 1.9 %copy.6 = bf16[128,2048]{1,0:T(8,128)(2,1)} copy(bf16[128,2048]{1,0:T(8,128)(2,1)} %relay_attention.1) | data formatting | bytes 1048576

commit v5 on v4

--- a/solution.py
+++ b/solution.py
@@ -233,41 +233,53 @@
                 keys = held[behind, heads + at, from_y, 0, from_c]
             return jnp.dot(keys, q_cols[heads + at, :, cols_of(part)], preferred_element_type=jnp.float32)
 
-        def fold(chain, scores):
+        def top_of(chain, scores):
             at, part = chain
-            head, cols = heads + at, cols_of(part)
+            cols = cols_of(part)
+            allowed = key_pos >= query_start[:, cols] - key_start
+            if first:
+                allowed = allowed & (key_pos <= query_pos[:, cols] - key_start)
+            scores = jnp.where(allowed, scores, masked_score)
+            best, rows = scores, count
+            while rows > 8:
+                rows //= 2
+                best = jnp.maximum(best[:rows], best[rows:])
+            return scores, jnp.max(best, axis=0, keepdims=True)
+
+        def values_of(chain):
+            head = heads + chain[0]
             if from_c is None:
                 values = jnp.concatenate(
                     [held[behind, head, from_y, 1, 0], held[behind, head, from_y, 1, 1]], axis=1
                 )
             else:
                 values = held[behind, head, from_y, 1, from_c]
-            allowed = key_pos >= query_start[:, cols] - key_start
+            return jnp.concatenate([values, jnp.ones((16, count), jnp.bfloat16)], axis=0)
+
+        masked = [top_of(chain, scores_of(chain)) for chain in chains]
+        highest, olds = [], []
+        for (at, part), (scores, top) in zip(chains, masked):
+            old_max = None if first else row_max[heads + at, :, cols_of(part)]
+            olds.append(old_max)
+            highest.append(top if first else jnp.maximum(old_max, top))
+        weights = [
+            jnp.exp2((scores - new_max) * EXP2_SCALE).astype(jnp.bfloat16)
+            for (scores, _), new_max in zip(masked, highest)
+        ]
+        mixed = [
+            jnp.dot(values_of(chain), weight, preferred_element_type=jnp.float32)
+            for chain, weight in zip(chains, weights)
+        ]
+        for (at, part), old_max, new_max, mix in zip(chains, olds, highest, mixed):
+            head, cols = heads + at, cols_of(part)
             if first:
-                allowed = allowed & (key_pos <= query_pos[:, cols] - key_start)
-            scores = jnp.where(allowed, scores, masked_score)
-            new_max = jnp.max(scores, axis=0, keepdims=True)
-            if not first:
-                old_max = row_max[head, :, cols]
-                new_max = jnp.maximum(old_max, new_max)
-            weights = jnp.exp2((scores - new_max) * EXP2_SCALE)
-            weight_sum = jnp.sum(weights, axis=0, keepdims=True)
-            mixed = jnp.dot(values, weights.astype(jnp.bfloat16), preferred_element_type=jnp.float32)
-            if first:
-                row_sum[head, :, cols] = weight_sum
-                total[head, :, cols] = mixed
+                row_sum[head, :, cols] = mix[HEAD_WIDTH:HEAD_WIDTH + 1]
+                total[head, :, cols] = mix[:HEAD_WIDTH]
             else:
                 factor = jnp.exp2((old_max - new_max) * EXP2_SCALE)
-                row_sum[head, :, cols] = row_sum[head, :, cols] * factor + weight_sum
-                total[head, :, cols] = total[head, :, cols] * factor + mixed
+                row_sum[head, :, cols] = row_sum[head, :, cols] * factor + mix[HEAD_WIDTH:HEAD_WIDTH + 1]
+                total[head, :, cols] = total[head, :, cols] * factor + mix[:HEAD_WIDTH]
             row_max[head, :, cols] = new_max
-
-        ready = scores_of(chains[0])
-        for number, chain in enumerate(chains):
-            scores = ready
-            if number + 1 < len(chains):
-                ready = scores_of(chains[number + 1])
-            fold(chain, scores)
 
     def each(heads, wait):
         for at in range(HEADS_AT_ONCE):
@@ -403,7 +415,7 @@
             for own in range(GROUP_HEADS):
                 own_cols = slice(own * tokens, (own + 1) * tokens)
                 columns = slice(own * HEAD_WIDTH, (own + 1) * HEAD_WIDTH)
-                o_rows[head, :, columns] = result[:, own_cols].T.astype(jnp.bfloat16)
+                o_rows[head, :, columns] = result[:, own_cols].astype(jnp.bfloat16).T
             o_copy(head).start()
 
     @pl.loop(0, KEY_VALUE_HEADS)
@@ -458,7 +470,7 @@
     pairs = 9 * tokens * tokens * QUERY_HEADS
     return pl.pallas_call(
         relay_kernel,
-        out_shape=jax.ShapeDtypeStruct(rotated_queries.shape, jnp.bfloat16),
+        out_shape=pltpu.VMEM(rotated_queries.shape, jnp.bfloat16),
         in_specs=[in_hbm] * 4,
         out_specs=pl.BlockSpec(memory_space=pl.ANY),
         scratch_shapes=[
@@ -480,7 +492,7 @@
             pltpu.SemaphoreType.DMA((HOPS, KEY_VALUE_HEADS)),
         ],
         compiler_params=pltpu.CompilerParams(
-            collective_id=0, has_side_effects=True, vmem_limit_bytes=64 * 1024 * 1024
+            collective_id=0, has_side_effects=True, vmem_limit_bytes=60 * 1024 * 1024
         ),
         cost_estimate=pl.CostEstimate(
             flops=4 * pairs * HEAD_WIDTH, bytes_accessed=4 * 1024 * 1024, transcendentals=pairs

time: 26.1 us -> 23.5 us (0.900)
  Pallas kernels: 24 us -> 22.6 us
  local copies, waits for them, and re-layouts: 1.88 us -> 0.8 us
    pallas_call x1, Pallas kernels: 24 us -> 22.6 us  [relay_attention(): pl.pallas_call(relay_kernel, out_shape=pltpu.VMEM(rotated_queries.shape,...]
    unnamed x1, local copies, waits for them, and re-layouts: 1.88 us -> 0.8 us
where the time goes in v5:
time: 23.5 us; the launch traced here: 23.4 us
  Pallas kernels  22.6 us (96%)
  local copies, waits for them, and re-layouts  0.8 us (3%)
    pallas_call x1, Pallas kernels, relay_attention(): pl.pallas_call(relay_kernel, out_shape=pltpu.VMEM(rotated_queries.shape,...  22.6 us
    unnamed x1, local copies, waits for them, and re-layouts  0.8 us

profile of v5, /device:TPU:17, one launch (start us, length us, event | category | flops | bytes accessed | tf_op | source)
XLA Modules:
  0.0 23.4 jit_solution(12448965706065062551)
XLA Ops:
  0.0 22.6 %relay_attention.1 = bf16[128,2048]{1,0:T(8,128)(2,1)S(1)} custom-call(s32[4]{0:T(128)} %lengths_hbm.1, bf16[128,2048]{1,0:T(8,128)(2,1)} %q_hbm.1, bf16[128,512]{1,0:T(8,128)(2,1)} %k_hbm.1, bf16[128,512]{1,0:T(8,128)(2,1)} %v_hbm.1), custom_call_target="tpu_custom_call" | custom-call | flops 1207959552 | bytes 4194304 | tf_op jit(solution)/shard_map/relay_attention/pallas_call | solution.py:471
  22.6 0.8 %copy.6 = bf16[128,2048]{1,0:T(8,128)(2,1)} copy(bf16[128,2048]{1,0:T(8,128)(2,1)S(1)} %relay_attention.1) | data formatting | bytes 1048576

commit v6 on v5

--- a/solution.py
+++ b/solution.py
@@ -100,7 +100,7 @@
 GROUP_HEADS = QUERY_HEADS // KEY_VALUE_HEADS
 EXP2_SCALE = math.log2(math.e) / math.sqrt(HEAD_WIDTH)
 
-(Z1, Z2, C0, C1, C2, YA, YB, CYA, CYB) = range(9)
+(Z1, Z2, YA, YB, C0, C1, CYA, C2, CYB) = range(9)
 HOPS = 9
 HEADS_AT_ONCE = 2
 
@@ -171,6 +171,20 @@
     def _():
         greet(down)
 
+    row_max[...] = jnp.full(row_max.shape, masked_score, jnp.float32)
+    row_sum[...] = jnp.zeros(row_sum.shape, jnp.float32)
+    total[...] = jnp.zeros(total.shape, jnp.float32)
+    for head in range(KEY_VALUE_HEADS):
+        blank = jnp.zeros((2, tokens, HEAD_WIDTH), jnp.bfloat16)
+
+        @pl.when(c == 0)
+        def _():
+            held[0, head, y, :, 1] = blank
+
+        @pl.when(c == 1)
+        def _():
+            held[2, head, y, :, 0] = blank
+
     for head in range(KEY_VALUE_HEADS):
         v_copy(head).wait()
         held[0, head, y, 1, c] = v_rows[head].astype(jnp.float32).T.astype(jnp.bfloat16)
@@ -217,9 +231,9 @@
     half = lanes // 2
     chains = [(at, part) for at in range(HEADS_AT_ONCE) for part in range(2)]
 
-    def attend(heads, behind, from_y, from_c, first=False):
-        count = tokens if from_c is not None else 2 * tokens
-        key_start = ((z - behind) * 4 + from_y * 2 + (0 if from_c is None else from_c)) * tokens
+    def attend(heads, behind, from_y):
+        count = 2 * tokens
+        key_start = ((z - behind) * 4 + from_y * 2) * tokens
         key_pos = lax.broadcasted_iota(jnp.int32, (count, half), 0)
 
         def cols_of(part):
@@ -227,18 +241,13 @@
 
         def scores_of(chain):
             at, part = chain
-            if from_c is None:
-                keys = held[behind, heads + at, from_y, 0].reshape(count, HEAD_WIDTH)
-            else:
-                keys = held[behind, heads + at, from_y, 0, from_c]
+            keys = held[behind, heads + at, from_y, 0].reshape(count, HEAD_WIDTH)
             return jnp.dot(keys, q_cols[heads + at, :, cols_of(part)], preferred_element_type=jnp.float32)
 
         def top_of(chain, scores):
             at, part = chain
             cols = cols_of(part)
-            allowed = key_pos >= query_start[:, cols] - key_start
-            if first:
-                allowed = allowed & (key_pos <= query_pos[:, cols] - key_start)
+            allowed = (key_pos >= query_start[:, cols] - key_start) & (key_pos <= query_pos[:, cols] - key_start)
             scores = jnp.where(allowed, scores, masked_score)
             best, rows = scores, count
             while rows > 8:
@@ -248,20 +257,17 @@
 
         def values_of(chain):
             head = heads + chain[0]
-            if from_c is None:
-                values = jnp.concatenate(
-                    [held[behind, head, from_y, 1, 0], held[behind, head, from_y, 1, 1]], axis=1
-                )
-            else:
-                values = held[behind, head, from_y, 1, from_c]
+            values = jnp.concatenate(
+                [held[behind, head, from_y, 1, 0], held[behind, head, from_y, 1, 1]], axis=1
+            )
             return jnp.concatenate([values, jnp.ones((16, count), jnp.bfloat16)], axis=0)
 
         masked = [top_of(chain, scores_of(chain)) for chain in chains]
         highest, olds = [], []
         for (at, part), (scores, top) in zip(chains, masked):
-            old_max = None if first else row_max[heads + at, :, cols_of(part)]
+            old_max = row_max[heads + at, :, cols_of(part)]
             olds.append(old_max)
-            highest.append(top if first else jnp.maximum(old_max, top))
+            highest.append(jnp.maximum(old_max, top))
         weights = [
             jnp.exp2((scores - new_max) * EXP2_SCALE).astype(jnp.bfloat16)
             for (scores, _), new_max in zip(masked, highest)
@@ -272,13 +278,9 @@
         ]
         for (at, part), old_max, new_max, mix in zip(chains, olds, highest, mixed):
             head, cols = heads + at, cols_of(part)
-            if first:
-                row_sum[head, :, cols] = mix[HEAD_WIDTH:HEAD_WIDTH + 1]
-                total[head, :, cols] = mix[:HEAD_WIDTH]
-            else:
-                factor = jnp.exp2((old_max - new_max) * EXP2_SCALE)
-                row_sum[head, :, cols] = row_sum[head, :, cols] * factor + mix[HEAD_WIDTH:HEAD_WIDTH + 1]
-                total[head, :, cols] = total[head, :, cols] * factor + mix[:HEAD_WIDTH]
+            factor = jnp.exp2((old_max - new_max) * EXP2_SCALE)
+            row_sum[head, :, cols] = row_sum[head, :, cols] * factor + mix[HEAD_WIDTH:HEAD_WIDTH + 1]
+            total[head, :, cols] = total[head, :, cols] * factor + mix[:HEAD_WIDTH]
             row_max[head, :, cols] = new_max
 
     def each(heads, wait):
@@ -328,95 +330,51 @@
         columns = pl.ds(pl.multiple_of(head * lanes, lanes), lanes)
         return pltpu.make_async_copy(o_rows.at[head], o_hbm.at[:, columns], o_sem.at[head])
 
-    @pl.loop(0, 2)
-    def _(step):
-        heads = step * HEADS_AT_ONCE
-
-        @pl.when(c == 0)
-        def _():
-            attend(heads, 0, y, 0, first=True)
-
-        @pl.when(c == 1)
-        def _():
-            each(heads, lambda head: arrived(C0, head, 0, y, 0))
-            attend(heads, 0, y, None, first=True)
-
-        z_first(step)
-
-    y_first(0)
-
-    @pl.loop(0, 2)
-    def _(step):
-        heads = step * HEADS_AT_ONCE
-
-        @pl.when(step == 0)
-        def _():
-            z_first(2)
-            y_first(1)
-
-        @pl.when(step == 1)
-        def _():
-            y_first(3)
-
-        @pl.when(z >= 1)
-        def _():
-            each(heads, lambda head: arrived(C1, head, 1, y, 1 - c))
-            attend(heads, 1, y, None)
-
-        @pl.when(step == 0)
-        def _():
-            z_first(3)
-            y_first(2)
-
-        @pl.when(step == 1)
-        def _():
-            z_second(0)
-
-        @pl.when(crosses_first)
-        def _():
-            each(heads, lambda head: arrived(CYA, head, 1 - y, 1 - y, 1 - c))
-            attend(heads, 1 - y, 1 - y, None)
-
-    z_second(1)
-    y_second(0)
-    z_second(2)
-    y_second(1)
-
-    @pl.loop(0, 2)
-    def _(step):
-        heads = step * HEADS_AT_ONCE
-
-        @pl.when((z >= 2) & (c == 0))
-        def _():
-            each(heads, lambda head: arrived(C2, head, 2, y, 1))
-            attend(heads, 2, y, None)
-
-        @pl.when((z >= 2) & (c == 1))
-        def _():
-            attend(heads, 2, y, 1)
-
-        @pl.when(step == 0)
-        def _():
-            z_second(3)
-            y_second(2)
-
-        @pl.when(step == 1)
-        def _():
-            y_second(3)
-
-        @pl.when(crosses_second)
-        def _():
-            each(heads, lambda head: arrived(CYB, head, 2 - y, 1 - y, 1 - c))
-            attend(heads, 2 - y, 1 - y, None)
-
-        for at in range(HEADS_AT_ONCE):
-            head = heads + at
-            result = total[head] * (1.0 / row_sum[head])
-            for own in range(GROUP_HEADS):
-                own_cols = slice(own * tokens, (own + 1) * tokens)
-                columns = slice(own * HEAD_WIDTH, (own + 1) * HEAD_WIDTH)
-                o_rows[head, :, columns] = result[:, own_cols].astype(jnp.bfloat16).T
-            o_copy(head).start()
+    ahead = {
+        1: [(z_first, 0)],
+        2: [(z_first, 1), (y_first, 0), (z_first, 2), (y_first, 1)],
+        3: [(z_first, 3), (y_first, 2)],
+        4: [(y_first, 3)],
+        5: [(z_second, 0)],
+        6: [(z_second, 1), (y_second, 0), (z_second, 2), (y_second, 1)],
+        7: [(z_second, 3), (y_second, 2)],
+        9: [(y_second, 3)],
+    }
+
+    @pl.loop(0, 10)
+    def _(item):
+        later = (item + 8) // 10
+        kind = later * (1 + (item + 8) % 2 + 2 * ((item + 8) // 14))
+        pair = (1 - later) * item + later * (((item + 8) // 2 + 1) % 2)
+        heads = pair * HEADS_AT_ONCE
+        crossed = (1 - kind % 2) * ((kind + 4) // 5)
+        behind = (kind + 1) // 2 - crossed * y
+        from_y = y + crossed * (1 - 2 * y)
+
+        for number, steps in ahead.items():
+            @pl.when(item == number)
+            def _():
+                for pass_on, head in steps:
+                    pass_on(head)
+
+        @pl.when(z >= behind)
+        def _():
+            @pl.when(((kind != 0) | (c == 1)) & ((kind != 3) | (c == 0)))
+            def _():
+                each(heads, lambda head: arrived(C0 + kind, head, behind, from_y, 1 - c))
+
+            attend(heads, behind, from_y)
+
+        @pl.when((item == 7) | (item == 9))
+        def _():
+            for at in range(HEADS_AT_ONCE):
+                head = heads + at
+                result = total[head] * (1.0 / row_sum[head])
+                for own in range(GROUP_HEADS):
+                    own_cols = slice(own * tokens, (own + 1) * tokens)
+                    columns = slice(own * HEAD_WIDTH, (own + 1) * HEAD_WIDTH)
+                    o_rows[head, :, columns] = result[:, own_cols].astype(jnp.bfloat16).T
+                o_copy(head).start()
 
     @pl.loop(0, KEY_VALUE_HEADS)
     def _(head):

time: 23.5 us -> 24.3 us (1.034)
  Pallas kernels: 22.6 us -> 23.3 us
    pallas_call x1, Pallas kernels: 22.6 us -> 23.3 us  [relay_attention(): pl.pallas_call(relay_kernel, out_shape=pltpu.VMEM(rotated_queries.shape,...]
where the time goes in v6:
time: 24.3 us; the launch traced here: 24.1 us
  Pallas kernels  23.3 us (96%)
  local copies, waits for them, and re-layouts  0.8 us (3%)
    pallas_call x1, Pallas kernels, relay_attention(): pl.pallas_call(relay_kernel, out_shape=pltpu.VMEM(rotated_queries.shape,...  23.3 us
    unnamed x1, local copies, waits for them, and re-layouts  0.8 us

profile of v6, /device:TPU:17, one launch (start us, length us, event | category | flops | bytes accessed | tf_op | source)
XLA Modules:
  0.0 24.1 jit_solution(13636661005009951857)
XLA Ops:
  0.0 23.3 %relay_attention.1 = bf16[128,2048]{1,0:T(8,128)(2,1)S(1)} custom-call(s32[4]{0:T(128)} %lengths_hbm.1, bf16[128,2048]{1,0:T(8,128)(2,1)} %q_hbm.1, bf16[128,512]{1,0:T(8,128)(2,1)} %k_hbm.1, bf16[128,512]{1,0:T(8,128)(2,1)} %v_hbm.1), custom_call_target="tpu_custom_call" | custom-call | flops 1207959552 | bytes 4194304 | tf_op jit(solution)/shard_map/relay_attention/pallas_call | solution.py:429
  23.3 0.8 %copy.6 = bf16[128,2048]{1,0:T(8,128)(2,1)} copy(bf16[128,2048]{1,0:T(8,128)(2,1)S(1)} %relay_attention.1) | data formatting | bytes 1048576

commit v7 on v5

--- a/solution.py
+++ b/solution.py
@@ -100,8 +100,8 @@
 GROUP_HEADS = QUERY_HEADS // KEY_VALUE_HEADS
 EXP2_SCALE = math.log2(math.e) / math.sqrt(HEAD_WIDTH)
 
-(Z1, Z2, C0, C1, C2, YA, YB, CYA, CYB) = range(9)
-HOPS = 9
+(Z1, Z2, C0, C1, C2, YA, YB, CYA, CYB, ZY) = range(10)
+HOPS = 10
 HEADS_AT_ONCE = 2
 
 
@@ -133,10 +133,10 @@
         columns = pl.ds(head * HEAD_WIDTH, HEAD_WIDTH)
         return pltpu.make_async_copy(v_hbm.at[:, columns], v_rows.at[head], v_sem.at[head])
 
-    def hop(kind, head, source, target, device):
+    def hop(kind, head, source, target, device, landing_kind=None):
         return pltpu.make_async_remote_copy(
             src_ref=source, dst_ref=target, send_sem=send_sem.at[kind, head],
-            recv_sem=recv_sem.at[kind, head], device_id=place(device), device_id_type=MESH,
+            recv_sem=recv_sem.at[kind if landing_kind is None else landing_kind, head], device_id=place(device), device_id_type=MESH,
         )
 
     def send(kind, head, behind, from_y, from_c, device, landing=None):
@@ -302,20 +302,27 @@
         def _():
             arrived(Z2, head, 2, y, c)
 
-            @pl.when(y == 1)
-            def _():
-                send(YB, head, 2, y, c, across)
+            if head < KEY_VALUE_HEADS - 1:
+                @pl.when(y == 1)
+                def _():
+                    send(YB, head, 2, y, c, across)
 
             @pl.when(c == 1)
             def _():
                 send(C2, head, 2, y, c, twin)
 
+    sends_last = (y == 0) & (z >= 1) & (z < 3)
     crosses_first, crosses_second = z + y >= 1, z + y >= 2
 
     def y_first(head):
         @pl.when(crosses_first)
         def _():
             arrived(YA, head, 1 - y, 1 - y, c)
+            if head == KEY_VALUE_HEADS - 1:
+                @pl.when(sends_last)
+                def _():
+                    hop(ZY, head, slot(1, head, 1, c), slot(2, head, 1, c), up, landing_kind=YB).start()
+
             send(CYA, head, 1 - y, 1 - y, c, twin)
 
     def y_second(head):
@@ -379,13 +386,16 @@
 
     z_second(1)
     y_second(0)
-    z_second(2)
-    y_second(1)
 
     @pl.loop(0, 2)
     def _(step):
         heads = step * HEADS_AT_ONCE
 
+        @pl.when(step == 1)
+        def _():
+            z_second(3)
+            y_second(2)
+
         @pl.when((z >= 2) & (c == 0))
         def _():
             each(heads, lambda head: arrived(C2, head, 2, y, 1))
@@ -397,8 +407,8 @@
 
         @pl.when(step == 0)
         def _():
-            z_second(3)
-            y_second(2)
+            z_second(2)
+            y_second(1)
 
         @pl.when(step == 1)
         def _():
@@ -438,9 +448,13 @@
         def _():
             sent(YA, y, y, c)
 
-        @pl.when(z - y >= 1)
+        @pl.when((z - y >= 1) & ((y == 0) | (head < KEY_VALUE_HEADS - 1)))
         def _():
             sent(YB, 1 + y, y, c)
+
+        @pl.when(sends_last & (head == KEY_VALUE_HEADS - 1))
+        def _():
+            sent(ZY, 1, 1, c)
 
         @pl.when(crosses_first)
         def _():

time: 23.5 us -> 24.2 us (1.030)
  Pallas kernels: 22.6 us -> 23.3 us
    pallas_call x1, Pallas kernels: 22.6 us -> 23.3 us  [relay_attention(): pl.pallas_call(relay_kernel, out_shape=pltpu.VMEM(rotated_queries.shape,...]
where the time goes in v7:
time: 24.2 us; the launch traced here: 24.1 us
  Pallas kernels  23.3 us (96%)
  local copies, waits for them, and re-layouts  0.8 us (3%)
    pallas_call x1, Pallas kernels, relay_attention(): pl.pallas_call(relay_kernel, out_shape=pltpu.VMEM(rotated_queries.shape,...  23.3 us
    unnamed x1, local copies, waits for them, and re-layouts  0.8 us

profile of v7, /device:TPU:17, one launch (start us, length us, event | category | flops | bytes accessed | tf_op | source)
XLA Modules:
  0.0 24.1 jit_solution(13350661981103903211)
XLA Ops:
  0.0 23.3 %relay_attention.1 = bf16[128,2048]{1,0:T(8,128)(2,1)S(1)} custom-call(s32[4]{0:T(128)} %lengths_hbm.1, bf16[128,2048]{1,0:T(8,128)(2,1)} %q_hbm.1, bf16[128,512]{1,0:T(8,128)(2,1)} %k_hbm.1, bf16[128,512]{1,0:T(8,128)(2,1)} %v_hbm.1), custom_call_target="tpu_custom_call" | custom-call | flops 1207959552 | bytes 4194304 | tf_op jit(solution)/shard_map/relay_attention/pallas_call | solution.py:485
  23.3 0.8 %copy.6 = bf16[128,2048]{1,0:T(8,128)(2,1)} copy(bf16[128,2048]{1,0:T(8,128)(2,1)S(1)} %relay_attention.1) | data formatting | bytes 1048576

commit v8 on v5

--- a/solution.py
+++ b/solution.py
@@ -122,8 +122,8 @@
     def place(device):
         return (group, device)
 
-    def slot(behind, head, from_y, from_c):
-        return held.at[behind, head, from_y, :, from_c]
+    def slot(behind, head, from_y, from_c, which):
+        return held.at[behind, head, from_y, which, from_c]
 
     def k_copy(head):
         columns = pl.ds(head * HEAD_WIDTH, HEAD_WIDTH)
@@ -133,19 +133,24 @@
         columns = pl.ds(head * HEAD_WIDTH, HEAD_WIDTH)
         return pltpu.make_async_copy(v_hbm.at[:, columns], v_rows.at[head], v_sem.at[head])
 
-    def hop(kind, head, source, target, device):
+    def hop(kind, head, which, source, target, device):
         return pltpu.make_async_remote_copy(
-            src_ref=source, dst_ref=target, send_sem=send_sem.at[kind, head],
-            recv_sem=recv_sem.at[kind, head], device_id=place(device), device_id_type=MESH,
+            src_ref=source, dst_ref=target, send_sem=send_sem.at[kind, head, which],
+            recv_sem=recv_sem.at[kind, head, which], device_id=place(device), device_id_type=MESH,
         )
 
-    def send(kind, head, behind, from_y, from_c, device, landing=None):
+    def send(kind, head, which, behind, from_y, from_c, device, landing=None):
         landing = behind if landing is None else landing
-        hop(kind, head, slot(behind, head, from_y, from_c), slot(landing, head, from_y, from_c), device).start()
+        source = slot(behind, head, from_y, from_c, which)
+        hop(kind, head, which, source, slot(landing, head, from_y, from_c, which), device).start()
+
+    def arrived_one(kind, head, which, behind, from_y, from_c):
+        here = slot(behind, head, from_y, from_c, which)
+        hop(kind, head, which, here, here, twin).wait_recv()
 
     def arrived(kind, head, behind, from_y, from_c):
-        here = slot(behind, head, from_y, from_c)
-        hop(kind, head, here, here, twin).wait_recv()
+        for which in range(2):
+            arrived_one(kind, head, which, behind, from_y, from_c)
 
     q_copy = pltpu.make_async_copy(q_hbm, q_rows, q_sem)
     lengths_copy = pltpu.make_async_copy(lengths_hbm, lengths, lengths_sem)
@@ -188,17 +193,18 @@
     for head in range(KEY_VALUE_HEADS):
         k_copy(head).wait()
 
-        @pl.when(z < 3)
-        def _():
-            send(Z1, head, 0, y, c, up, landing=1)
-
-        @pl.when(y == 0)
-        def _():
-            send(YA, head, 0, y, c, across)
-
-        @pl.when(c == 0)
-        def _():
-            send(C0, head, 0, y, c, twin)
+        for which in range(2):
+            @pl.when(z < 3)
+            def _():
+                send(Z1, head, which, 0, y, c, up, landing=1)
+
+            @pl.when(y == 0)
+            def _():
+                send(YA, head, which, 0, y, c, across)
+
+            @pl.when(c == 0)
+            def _():
+                send(C0, head, which, 0, y, c, twin)
 
     lengths_copy.wait()
     q_copy.wait()
@@ -288,41 +294,45 @@
     def z_first(head):
         @pl.when(z >= 1)
         def _():
-            arrived(Z1, head, 1, y, c)
-
-            @pl.when(z < 3)
-            def _():
-                send(Z2, head, 1, y, c, up, landing=2)
-
-            send(YB - y, head, 1, y, c, across)
-            send(C1, head, 1, y, c, twin)
+            for which in range(2):
+                arrived_one(Z1, head, which, 1, y, c)
+
+                @pl.when(z < 3)
+                def _():
+                    send(Z2, head, which, 1, y, c, up, landing=2)
+
+                send(YB - y, head, which, 1, y, c, across)
+                send(C1, head, which, 1, y, c, twin)
 
     def z_second(head):
         @pl.when(z >= 2)
         def _():
-            arrived(Z2, head, 2, y, c)
-
-            @pl.when(y == 1)
-            def _():
-                send(YB, head, 2, y, c, across)
-
-            @pl.when(c == 1)
-            def _():
-                send(C2, head, 2, y, c, twin)
+            for which in range(2):
+                arrived_one(Z2, head, which, 2, y, c)
+
+                @pl.when(y == 1)
+                def _():
+                    send(YB, head, which, 2, y, c, across)
+
+                @pl.when(c == 1)
+                def _():
+                    send(C2, head, which, 2, y, c, twin)
 
     crosses_first, crosses_second = z + y >= 1, z + y >= 2
 
     def y_first(head):
         @pl.when(crosses_first)
         def _():
-            arrived(YA, head, 1 - y, 1 - y, c)
-            send(CYA, head, 1 - y, 1 - y, c, twin)
+            for which in range(2):
+                arrived_one(YA, head, which, 1 - y, 1 - y, c)
+                send(CYA, head, which, 1 - y, 1 - y, c, twin)
 
     def y_second(head):
         @pl.when(crosses_second)
         def _():
-            arrived(YB, head, 2 - y, 1 - y, c)
-            send(CYB, head, 2 - y, 1 - y, c, twin)
+            for which in range(2):
+                arrived_one(YB, head, which, 2 - y, 1 - y, c)
+                send(CYB, head, which, 2 - y, 1 - y, c, twin)
 
     def o_copy(head):
         columns = pl.ds(pl.multiple_of(head * lanes, lanes), lanes)
@@ -423,8 +433,9 @@
         o_copy(head).wait()
 
         def sent(kind, behind, from_y, from_c):
-            here = slot(behind, head, from_y, from_c)
-            hop(kind, head, here, here, twin).wait_send()
+            for which in range(2):
+                here = slot(behind, head, from_y, from_c, which)
+                hop(kind, head, which, here, here, twin).wait_send()
 
         @pl.when(z < 3)
         def _():
@@ -488,8 +499,8 @@
             pltpu.SemaphoreType.DMA((KEY_VALUE_HEADS,)),
             pltpu.SemaphoreType.DMA,
             pltpu.SemaphoreType.DMA((KEY_VALUE_HEADS,)),
-            pltpu.SemaphoreType.DMA((HOPS, KEY_VALUE_HEADS)),
-            pltpu.SemaphoreType.DMA((HOPS, KEY_VALUE_HEADS)),
+            pltpu.SemaphoreType.DMA((HOPS, KEY_VALUE_HEADS, 2)),
+            pltpu.SemaphoreType.DMA((HOPS, KEY_VALUE_HEADS, 2)),
         ],
         compiler_params=pltpu.CompilerParams(
             collective_id=0, has_side_effects=True, vmem_limit_bytes=60 * 1024 * 1024

time: 23.5 us -> 24.1 us (1.026)
  Pallas kernels: 22.6 us -> 23.2 us
    pallas_call x1, Pallas kernels: 22.6 us -> 23.2 us  [relay_attention(): pl.pallas_call(relay_kernel, out_shape=pltpu.VMEM(rotated_queries.shape,...]
where the time goes in v8:
time: 24.1 us; the launch traced here: 24 us
  Pallas kernels  23.2 us (96%)
  local copies, waits for them, and re-layouts  0.8 us (3%)
    pallas_call x1, Pallas kernels, relay_attention(): pl.pallas_call(relay_kernel, out_shape=pltpu.VMEM(rotated_queries.shape,...  23.2 us
    unnamed x1, local copies, waits for them, and re-layouts  0.8 us

profile of v8, /device:TPU:17, one launch (start us, length us, event | category | flops | bytes accessed | tf_op | source)
XLA Modules:
  0.0 24.0 jit_solution(6304858841015116408)
XLA Ops:
  0.0 23.2 %relay_attention.1 = bf16[128,2048]{1,0:T(8,128)(2,1)S(1)} custom-call(s32[4]{0:T(128)} %lengths_hbm.1, bf16[128,2048]{1,0:T(8,128)(2,1)} %q_hbm.1, bf16[128,512]{1,0:T(8,128)(2,1)} %k_hbm.1, bf16[128,512]{1,0:T(8,128)(2,1)} %v_hbm.1), custom_call_target="tpu_custom_call" | custom-call | flops 1207959552 | bytes 4194304 | tf_op jit(solution)/shard_map/relay_attention/pallas_call | solution.py:482
  23.2 0.8 %copy.6 = bf16[128,2048]{1,0:T(8,128)(2,1)} copy(bf16[128,2048]{1,0:T(8,128)(2,1)S(1)} %relay_attention.1) | data formatting | bytes 1048576

commit v9 on v5

--- a/solution.py
+++ b/solution.py
@@ -106,9 +106,9 @@
 
 
 def relay_kernel(
-    lengths_hbm, q_hbm, k_hbm, v_hbm, o_hbm,
-    lengths, held, q_rows, v_rows, q_cols, row_max, row_sum, total, o_rows,
-    lengths_sem, k_sem, v_sem, q_sem, o_sem, send_sem, recv_sem,
+    lengths_hbm, q_hbm, k_hbm, v_hbm, o_ref,
+    lengths, held, q_rows, v_rows, q_cols, row_max, row_sum, total,
+    lengths_sem, k_sem, v_sem, q_sem, send_sem, recv_sem,
 ):
     tokens = q_hbm.shape[0]
     lanes = GROUP_HEADS * tokens
@@ -324,10 +324,6 @@
             arrived(YB, head, 2 - y, 1 - y, c)
             send(CYB, head, 2 - y, 1 - y, c, twin)
 
-    def o_copy(head):
-        columns = pl.ds(pl.multiple_of(head * lanes, lanes), lanes)
-        return pltpu.make_async_copy(o_rows.at[head], o_hbm.at[:, columns], o_sem.at[head])
-
     @pl.loop(0, 2)
     def _(step):
         heads = step * HEADS_AT_ONCE
@@ -414,14 +410,11 @@
             result = total[head] * (1.0 / row_sum[head])
             for own in range(GROUP_HEADS):
                 own_cols = slice(own * tokens, (own + 1) * tokens)
-                columns = slice(own * HEAD_WIDTH, (own + 1) * HEAD_WIDTH)
-                o_rows[head, :, columns] = result[:, own_cols].astype(jnp.bfloat16).T
-            o_copy(head).start()
+                first_column = pl.multiple_of((head * GROUP_HEADS + own) * HEAD_WIDTH, HEAD_WIDTH)
+                o_ref[:, pl.ds(first_column, HEAD_WIDTH)] = result[:, own_cols].astype(jnp.bfloat16).T
 
     @pl.loop(0, KEY_VALUE_HEADS)
     def _(head):
-        o_copy(head).wait()
-
         def sent(kind, behind, from_y, from_c):
             here = slot(behind, head, from_y, from_c)
             hop(kind, head, here, here, twin).wait_send()
@@ -472,7 +465,7 @@
         relay_kernel,
         out_shape=pltpu.VMEM(rotated_queries.shape, jnp.bfloat16),
         in_specs=[in_hbm] * 4,
-        out_specs=pl.BlockSpec(memory_space=pl.ANY),
+        out_specs=pl.BlockSpec(memory_space=pltpu.VMEM),
         scratch_shapes=[
             pltpu.SMEM(doc_lengths.shape, jnp.int32),
             pltpu.VMEM((3, KEY_VALUE_HEADS, 2, 2, 2, tokens, HEAD_WIDTH), jnp.bfloat16),
@@ -482,12 +475,10 @@
             pltpu.VMEM((KEY_VALUE_HEADS, 1, lanes), jnp.float32),
             pltpu.VMEM((KEY_VALUE_HEADS, 1, lanes), jnp.float32),
             pltpu.VMEM((KEY_VALUE_HEADS, HEAD_WIDTH, lanes), jnp.float32),
-            pltpu.VMEM((KEY_VALUE_HEADS, tokens, GROUP_HEADS * HEAD_WIDTH), jnp.bfloat16),
             pltpu.SemaphoreType.DMA,
             pltpu.SemaphoreType.DMA((KEY_VALUE_HEADS,)),
             pltpu.SemaphoreType.DMA((KEY_VALUE_HEADS,)),
             pltpu.SemaphoreType.DMA,
-            pltpu.SemaphoreType.DMA((KEY_VALUE_HEADS,)),
             pltpu.SemaphoreType.DMA((HOPS, KEY_VALUE_HEADS)),
             pltpu.SemaphoreType.DMA((HOPS, KEY_VALUE_HEADS)),
         ],

time: 23.5 us -> 23.4 us (level)
  no operation moved by 1% of the time
where the time goes in v9:
time: 23.4 us; the launch traced here: 23.2 us
  Pallas kernels  22.4 us (96%)
  local copies, waits for them, and re-layouts  0.8 us (3%)
    pallas_call x1, Pallas kernels, relay_attention(): pl.pallas_call(relay_kernel, out_shape=pltpu.VMEM(rotated_queries.shape,...  22.4 us
    unnamed x1, local copies, waits for them, and re-layouts  0.8 us

profile of v9, /device:TPU:17, one launch (start us, length us, event | category | flops | bytes accessed | tf_op | source)
XLA Modules:
  0.0 23.2 jit_solution(13465647555326346431)
XLA Ops:
  0.0 22.4 %relay_attention.1 = bf16[128,2048]{1,0:T(8,128)(2,1)S(1)} custom-call(s32[4]{0:T(128)} %lengths_hbm.1, bf16[128,2048]{1,0:T(8,128)(2,1)} %q_hbm.1, bf16[128,512]{1,0:T(8,128)(2,1)} %k_hbm.1, bf16[128,512]{1,0:T(8,128)(2,1)} %v_hbm.1), custom_call_target="tpu_custom_call" | custom-call | flops 1207959552 | bytes 4194304 | tf_op jit(solution)/shard_map/relay_attention/pallas_call | solution.py:464
  22.4 0.8 %copy.6 = bf16[128,2048]{1,0:T(8,128)(2,1)} copy(bf16[128,2048]{1,0:T(8,128)(2,1)S(1)} %relay_attention.1) | data formatting | bytes 1048576
